TPU v7x, 32 devices: a whole 2x2x4 slice. The times are simulated.
32 devices in a mesh: fsdp: 4 (over z), seq: 8 (over y, x, core).
Axes of the slice: x: 2, y: 2, z: 4, core: 2. Of those that a mesh axis runs over, the one named last changes fastest.
Arguments:
- tokens: bfloat16 [4, 1024, 1024], P('fsdp', 'seq'), may hold values from -6 to 6
- segment_ids: int32 [4, 1024], P('fsdp'), may hold values from 0 to 2, as said below
- w_qkv: bfloat16 [1024, 3072], P('fsdp'), may hold values from -0.1875 to 0.1875
- w_attn_out: bfloat16 [1024, 1024], P('fsdp'), may hold values from -1.25 to 1.25
- w_in: bfloat16 [1024, 2, 2624], P('fsdp'), may hold values from -0.1875 to 0.1875
- w_mlp_out: bfloat16 [2624, 1024], P(None, 'fsdp'), may hold values from -0.125 to 0.125
- norm_gains: bfloat16 [2, 1024], P(None, 'fsdp'), may hold values from 0.5 to 1.5
- cotangent: bfloat16 [4, 1024, 1024], P('fsdp', 'seq'), may hold values from -6 to 6
Outputs:
- outputs: bfloat16 [4, 1024, 1024], P('fsdp', 'seq')
- input_grad: float32 [4, 1024, 1024], P('fsdp', 'seq')
- grad_w_qkv: float32 [1024, 3072], P(('fsdp', 'seq'))
- grad_w_attn_out: float32 [1024, 1024], P(('fsdp', 'seq'))
- grad_w_in: float32 [1024, 2, 2624], P(('fsdp', 'seq'))
- grad_w_mlp_out: float32 [2624, 1024], P(None, ('fsdp', 'seq'))
- grad_norm_gains: float32 [2, 1024], P(None, ('fsdp', 'seq'))
Inputs may be any that keep to these rules, and one draw needn't show every extreme that they name: `segment_ids`: each sequence holds at most three documents, numbered from 0 in order, so ids never fall along a sequence. No document boundary lies within 256 tokens of a sequence's ends or within 128 tokens of its middle.
All inputs are finite; a program needn't handle non-finite values.
Results may differ from a plain program's by a relative error of at most 0.014.
Values may be sent and summed in bfloat16 or wider, within the bound.
A program may use at most 256 MiB of HBM per device.

v0:
```python
import jax
import jax.numpy as jnp
from jax import lax
from jax.sharding import PartitionSpec as P

HEADS = 16
HD = 64
WIN = 128


norm_eps = 1e-05
rope_base = 10000.0
masked_score = -1e30


def padded(cells, sides, width):
    for axis, dim in sides:
        count = lax.axis_size(axis)
        ends = count - 1
        head = lax.slice_in_dim(cells, 0, width, axis=dim)
        tail = lax.slice_in_dim(cells, cells.shape[dim] - width, cells.shape[dim], axis=dim)
        cells = jnp.concatenate(
            [
                lax.ppermute(tail, axis, [(i, (i + 1) % count) for i in range(ends)]),
                cells,
                lax.ppermute(head, axis, [((i + 1) % count, i) for i in range(ends)]),
            ],
            axis=dim,
        )
    return cells


def layer_norm(values, norm_gain):
    centre = values - jnp.mean(values, axis=-1, keepdims=True)
    spread = jnp.mean(centre * centre, axis=-1, keepdims=True)
    return centre * lax.rsqrt(spread + norm_eps) * norm_gain


def rope_tables(positions, head_dim):
    half_dim = head_dim // 2
    inv_freq = rope_base ** (-(2.0 * jnp.arange(half_dim, dtype=jnp.float32)) / head_dim)
    angles = positions.astype(jnp.float32)[:, None] * inv_freq[None, :]
    return (jnp.cos(angles), jnp.sin(angles))


def rotate(values, cos_table, sin_table, head_count):
    tok_rows = values.shape[0]
    shaped = values.reshape(tok_rows, head_count, -1)
    half_dim = shaped.shape[-1] // 2
    first_half = shaped[..., :half_dim]
    second = shaped[..., half_dim:]
    cos_part = cos_table[:, None, :]
    sin_part = sin_table[:, None, :]
    turned = jnp.concatenate(
        [first_half * cos_part - second * sin_part, second * cos_part + first_half * sin_part],
        axis=-1,
    )
    return turned.reshape(tok_rows, -1)


def gated_gelu(upward):
    return jax.nn.gelu(upward[:, 0], approximate=False) * upward[:, 1]


def local(tokens, segment_ids, w_qkv, w_attn_out, w_in, w_mlp_out, norm_gains, cotangent):
    tok_rows = tokens.shape[1]
    model_width = tokens.shape[2]
    half_win = WIN // 2
    score_scale = HD ** (-0.5)
    row_start = lax.axis_index("seq") * tok_rows
    full_qkv, full_out, full_in, full_mlp, full_gains = (
        lax.all_gather(w_qkv, "fsdp", axis=0, tiled=True),
        lax.all_gather(w_attn_out, "fsdp", axis=0, tiled=True),
        lax.all_gather(w_in, "fsdp", axis=0, tiled=True),
        lax.all_gather(w_mlp_out, "fsdp", axis=1, tiled=True),
        lax.all_gather(norm_gains, "fsdp", axis=1, tiled=True),
    )
    gain_pair = full_gains.astype(jnp.float32)
    inputs = tokens[0].astype(jnp.float32)
    cos_table, sin_table = rope_tables(row_start + jnp.arange(tok_rows, dtype=jnp.int32), HD)
    h_one, norm_one_back = jax.vjp(layer_norm, inputs, gain_pair[0])
    a_one = h_one.astype(jnp.bfloat16)
    qkv_full = jnp.dot(a_one, full_qkv, preferred_element_type=jnp.float32)
    query_rows = rotate(qkv_full[:, :model_width], cos_table, sin_table, HEADS).astype(jnp.bfloat16)
    key_rows = rotate(
        qkv_full[:, model_width : 2 * model_width], cos_table, sin_table, HEADS
    ).astype(jnp.bfloat16)
    value_rows = qkv_full[:, 2 * model_width :].astype(jnp.bfloat16)
    kv_wide = padded(jnp.concatenate([key_rows, value_rows], axis=1), (("seq", 0),), half_win)
    key_wide = kv_wide[:, :model_width].reshape(-1, HEADS, HD)
    value_wide = kv_wide[:, model_width:].reshape(-1, HEADS, HD)
    row_ids = segment_ids[0]
    ids_pad = jnp.pad(row_ids, (half_win, half_win), constant_values=-1)
    k_ids = lax.dynamic_slice_in_dim(ids_pad, row_start, tok_rows + 2 * half_win)
    q_ids = lax.dynamic_slice_in_dim(row_ids, row_start, tok_rows)
    offsets = (
        jnp.arange(tok_rows)[:, None] - jnp.arange(tok_rows + 2 * half_win)[None, :] + half_win
    )
    allowed = (jnp.abs(offsets) <= half_win) & (q_ids[:, None] == k_ids[None, :])
    q_heads = query_rows.reshape(tok_rows, HEADS, HD)
    scores = (
        jnp.einsum("thd,shd->hts", q_heads, key_wide, preferred_element_type=jnp.float32)
        * score_scale
    )
    scores = jnp.where(allowed[None], scores, masked_score)
    row_max = jnp.max(scores, axis=-1, keepdims=True)
    exponent = jnp.exp(scores - row_max)
    row_sum = jnp.sum(exponent, axis=-1, keepdims=True)
    log_total = row_max + jnp.log(row_sum)
    attn_pb = (exponent / row_sum).astype(jnp.bfloat16)
    attn_o = jnp.einsum("hts,shd->thd", attn_pb, value_wide, preferred_element_type=jnp.float32)
    attn_ob = attn_o.reshape(tok_rows, model_width).astype(jnp.bfloat16)
    residual = inputs + jnp.dot(attn_ob, full_out, preferred_element_type=jnp.float32)
    h_two, norm_two_back = jax.vjp(layer_norm, residual, gain_pair[1])
    a_two = h_two.astype(jnp.bfloat16)
    upward = jnp.einsum("td,dcf->tcf", a_two, full_in, preferred_element_type=jnp.float32)
    middle, gelu_back = jax.vjp(gated_gelu, upward)
    middle_b = middle.astype(jnp.bfloat16)
    outputs = (residual + jnp.dot(middle_b, full_mlp, preferred_element_type=jnp.float32)).astype(
        jnp.bfloat16
    )
    back_qkv, back_out, back_in, back_mlp = (full_qkv, full_out, full_in, full_mlp)
    grad_out = cotangent[0].astype(jnp.float32)
    grad_mlp_b = grad_out.astype(jnp.bfloat16)
    grad_mid = jnp.einsum("td,fd->tf", grad_mlp_b, back_mlp, preferred_element_type=jnp.float32)
    grad_up_b = gelu_back(grad_mid)[0].astype(jnp.bfloat16)
    grad_a_two = jnp.einsum("tcf,dcf->td", grad_up_b, back_in, preferred_element_type=jnp.float32)
    grad_res_norm, grad_gain_two = norm_two_back(grad_a_two)
    grad_res = grad_out + grad_res_norm
    grad_att_b = grad_res.astype(jnp.bfloat16)
    grad_o_b = jnp.einsum(
        "te,de->td", grad_att_b, back_out, preferred_element_type=jnp.float32
    ).astype(jnp.bfloat16)
    grad_o_heads = grad_o_b.reshape(tok_rows, HEADS, HD)
    scores_again = (
        jnp.einsum("thd,shd->hts", q_heads, key_wide, preferred_element_type=jnp.float32)
        * score_scale
    )
    scores_again = jnp.where(allowed[None], scores_again, masked_score)
    prob_again = jnp.exp(scores_again - log_total)
    grad_prob = jnp.einsum(
        "thd,shd->hts", grad_o_heads, value_wide, preferred_element_type=jnp.float32
    )
    delta_sum = jnp.sum(grad_prob * prob_again, axis=-1, keepdims=True)
    grad_scores_b = (prob_again * (grad_prob - delta_sum)).astype(jnp.bfloat16)
    grad_query = (
        jnp.einsum("hts,shd->thd", grad_scores_b, key_wide, preferred_element_type=jnp.float32)
        * score_scale
    )
    grad_key_wide = (
        jnp.einsum("hts,thd->shd", grad_scores_b, q_heads, preferred_element_type=jnp.float32)
        * score_scale
    )
    grad_value_wide = jnp.einsum(
        "hts,thd->shd", attn_pb, grad_o_heads, preferred_element_type=jnp.float32
    )
    grad_kv_wide = jnp.concatenate(
        [grad_key_wide.reshape(-1, model_width), grad_value_wide.reshape(-1, model_width)], axis=1
    )
    rim_grads = jnp.concatenate(
        [grad_kv_wide[:half_win], grad_kv_wide[tok_rows + half_win :]], axis=0
    )
    arrived = padded(rim_grads.astype(jnp.bfloat16), (("seq", 0),), half_win).astype(
        rim_grads.dtype
    )
    own_grads = grad_kv_wide[half_win : half_win + tok_rows]
    own_grads = own_grads + jnp.pad(arrived[:half_win], ((0, tok_rows - half_win), (0, 0)))
    own_grads = own_grads + jnp.pad(arrived[3 * half_win :], ((tok_rows - half_win, 0), (0, 0)))
    grad_qkv_b = jnp.concatenate(
        [
            rotate(grad_query.reshape(tok_rows, model_width), cos_table, -sin_table, HEADS),
            rotate(own_grads[:, :model_width], cos_table, -sin_table, HEADS),
            own_grads[:, model_width:],
        ],
        axis=1,
    ).astype(jnp.bfloat16)
    grad_a_one = jnp.einsum("te,de->td", grad_qkv_b, back_qkv, preferred_element_type=jnp.float32)
    grad_in_norm, grad_gain_one = norm_one_back(grad_a_one)
    input_grad = grad_res + grad_in_norm
    gains_cols = jnp.stack([grad_gain_one, grad_gain_two], axis=1)
    grad_up_flat = grad_up_b.reshape(tok_rows, -1)
    ff_width = grad_mid.shape[1]
    summed = lax.psum_scatter(
        jnp.concatenate(
            [
                jnp.einsum("td,te->de", a_one, grad_qkv_b, preferred_element_type=jnp.float32),
                jnp.einsum("td,te->de", attn_ob, grad_att_b, preferred_element_type=jnp.float32),
                jnp.einsum("td,te->de", a_two, grad_up_flat, preferred_element_type=jnp.float32),
                jnp.einsum("td,tf->df", grad_mlp_b, middle_b, preferred_element_type=jnp.float32),
                gains_cols,
            ],
            axis=1,
        ),
        ("fsdp", "seq"),
        scatter_dimension=0,
        tiled=True,
    )
    own_rows = summed.shape[0]
    edge_one = 3 * model_width
    edge_two = edge_one + model_width
    edge_three = edge_two + 2 * ff_width
    edge_four = edge_three + ff_width
    sum_qkv = summed[:, :edge_one]
    sum_out = summed[:, edge_one:edge_two]
    sum_in = summed[:, edge_two:edge_three].reshape(own_rows, 2, ff_width)
    sum_mlp = summed[:, edge_three:edge_four].T
    sum_gains = summed[:, edge_four:].T
    return (outputs[None], input_grad[None], sum_qkv, sum_out, sum_in, sum_mlp, sum_gains)


def solution(mesh):
    return jax.shard_map(
        local,
        mesh=mesh,
        in_specs=(
            P("fsdp", "seq", None),
            P("fsdp", None),
            P("fsdp", None),
            P("fsdp", None),
            P("fsdp", None, None),
            P(None, "fsdp"),
            P(None, "fsdp"),
            P("fsdp", "seq", None),
        ),
        out_specs=(
            P("fsdp", "seq", None),
            P("fsdp", "seq", None),
            P(("fsdp", "seq"), None),
            P(("fsdp", "seq"), None),
            P(("fsdp", "seq"), None, None),
            P(None, ("fsdp", "seq")),
            P(None, ("fsdp", "seq")),
        ),
        check_vma=False,
    )
```

profile of v0, /device:TPU:0, one launch (start us, length us, event | category | flops | bytes accessed | tf_op | source)
XLA Modules:
  0.0 1108.3 jit_solution(2698447129615722559)
XLA Ops:
  7.2 0.7 all-gather.5.cloned.1.call-update
  7.9 0.7 all-gather.11.cloned.1.call-update
  8.7 0.7 all-gather.7.cloned.1.call-update
  10.1 12.6 %all_gather.15 = bf16[2,1024]{1,0:T(2,128)(2,1)S(1)} all-gather(bf16[2,256]{1,0:T(2,128)(2,1)S(1)} %copy-done.25), channel_id=1, replica_groups=mesh['fsdp'=4,'seq'=8] {'fsdp'}, dimensions={1}, use_global_device_ids=true | all-gather | bytes 5120 | tf_op jit(solution)/shard_map/all_gather | solution.py:76
  23.4 104.2 %all-gather.5.cloned.1.call-done = bf16[1024,3072]{1,0:T(8,128)(2,1)} async-done(((bf16[256,3072]{1,0:T(8,128)(2,1)}), bf16[1024,3072]{1,0:T(8,128)(2,1)}) %all-gather.5.cloned.1.call-update) | async-done | bytes 6291472 | tf_op jit(solution)/shard_map/all_gather | solution.py:72
  127.7 3.9 fusion.131
  132.0 0.8 subtract_convert_fusion.2
  133.1 2.0 collective-permute-start
  135.1 1.3 collective-permute-start.1
  136.4 91.0 %all-gather.11.cloned.1.call-done = bf16[2624,1024]{1,0:T(8,128)(2,1)} async-done(((bf16[2624,256]{1,0:T(8,128)(2,1)}), bf16[2624,1024]{1,0:T(8,128)(2,1)}) %all-gather.11.cloned.1.call-update) | async-done | bytes 5373968 | tf_op jit(solution)/shard_map/all_gather | solution.py:75
  227.3 5.2 fusion.87
  233.1 1.6 fusion.141
  235.4 0.9 divide_convert_fusion
  236.3 1.0 copy-done.7
  237.2 1.2 convolution_convert_fusion.1
  238.4 34.6 %all-gather.7.cloned.1.call-done = bf16[1024,1024]{1,0:T(8,128)(2,1)} async-done(((bf16[256,1024]{1,0:T(8,128)(2,1)}), bf16[1024,1024]{1,0:T(8,128)(2,1)}) %all-gather.7.cloned.1.call-update) | async-done | bytes 2097168 | tf_op jit(solution)/shard_map/all_gather | solution.py:73
  273.1 2.2 fusion.142
  275.5 185.4 %all-gather.9.cloned.1.call-done = bf16[1024,2,2624]{0,2,1:T(8,128)(2,1)} async-done(((bf16[256,2,2624]{0,2,1:T(8,128)(2,1)}), bf16[1024,2,2624]{0,2,1:T(8,128)(2,1)}) %all-gather.9.cloned.1.call-update) | async-done | bytes 10747920 | tf_op jit(solution)/shard_map/all_gather | solution.py:74
  460.9 6.0 fusion.89
  467.0 7.5 convolution_bitcast_fusion
  474.4 2.9 multiply_bitcast_fusion
  478.6 1.7 multiply_reduce_fusion.1
  480.7 0.8 copy-done.10
  481.6 2.6 fusion.144
  484.2 1.6 convolution_convert_fusion
  485.8 1.8 copy.34
  487.6 2.6 fusion.143
  490.2 1.1 copy.38
  491.2 1.8 multiply_reduce_fusion
  493.1 1.0 multiply_convert_fusion
  494.4 0.9 copy-done.8
  495.7 2.0 collective-permute-start.2
  497.8 1.3 collective-permute-start.3
  499.1 8.9 fusion.134
  508.5 0.7 maximum_convert_fusion
  509.8 0.7 fusion.38
  510.8 6.5 fusion.83
  517.3 2.4 fusion.81
  520.9 57.2 %concatenate.47 = f32[1024,11970]{1,0:T(8,128)} concatenate(f32[1024,3072]{1,0:T(8,128)} %fusion.83, f32[1024,1024]{1,0:T(8,128)} %fusion.144, f32[1024,5248]{1,0:T(8,128)} %fusion.134, f32[1024,2624]{1,0:T(8,128)} %convolution_bitcast_fusion, f32[1024,1]{1,0:T(8,128)S(1)} %copy.37, f32[1024,1]{1,0:T(8,128)S(1)} %copy-done.19), dimensions={1} | concatenate | bytes 98058240 | tf_op jit(solution)/shard_map/concatenate | solution.py:184
  578.1 1.7 copy-done.1
  579.8 4.7 fusion.35
  584.5 1.1 add_bitcast_fusion
  585.6 511.1 %reduce-scatter.2.cloned.1.call-done = f32[32,11970]{1,0:T(8,128)} async-done(((f32[1024,11970]{1,0:T(8,128)}), f32[32,11970]{1,0:T(8,128)}) %reduce-scatter.2.cloned.1.call-update) | async-done | bytes 1532176 | tf_op jit(solution)/shard_map/reduce_scatter | solution.py:183
  1096.7 0.9 slice_bitcast_fusion.1
  1098.2 1.4 reshape.272
  1099.6 0.7 slice.159
  1100.3 0.8 slice_bitcast_fusion
  1101.0 0.8 slice.158
  (122 shorter events, 9.3 us)
Async XLA Ops:
  7.2 120.5 %all-gather.5.cloned.1.call-start = ((), (), s32[]{:S(2)}) async-start(), calls=%async_computation.1 | async-start | bytes 7864320 | tf_op jit(solution)/shard_map/all_gather | solution.py:72
  7.9 219.4 %all-gather.11.cloned.1.call-start = ((), (), s32[]{:S(2)}) async-start(), calls=%async_computation.4 | async-start | bytes 6717440 | tf_op jit(solution)/shard_map/all_gather | solution.py:75
  8.7 264.4 %all-gather.7.cloned.1.call-start = ((), (), s32[]{:S(2)}) async-start(), calls=%async_computation.2 | async-start | bytes 2621440 | tf_op jit(solution)/shard_map/all_gather | solution.py:73
  9.4 0.7 copy-start.25
  9.4 13.3 %copy-start.24 = (s32[1,1024]{1,0:T(1,128)S(1)}, s32[1,1024]{1,0:T(1,128)}, u32[]{:S(2)}) copy-start(s32[1,1024]{1,0:T(1,128)} %param.9) | copy-start | bytes 12292
  9.4 13.4 %copy-start.4 = (bf16[1,128,1024]{2,1,0:T(8,128)(2,1)S(1)}, bf16[1,128,1024]{2,1,0:T(8,128)(2,1)}, u32[]{:S(2)}) copy-start(bf16[1,128,1024]{2,1,0:T(8,128)(2,1)} %param.8) | copy-start | bytes 786436
  9.4 451.5 %all-gather.9.cloned.1.call-start = ((), (), s32[]{:S(2)}) async-start(), calls=%async_computation.3 | async-start | bytes 13434880 | tf_op jit(solution)/shard_map/all_gather | solution.py:74
  10.0 1086.7 %reduce-scatter.2.cloned.1.call-start = ((), (), s32[]{:S(2)}) async-start(), calls=%async_computation.5 | async-start | bytes 50823168 | tf_op jit(solution)/shard_map/reduce_scatter | solution.py:183
  132.9 94.5 %copy-start.14 = (bf16[1,128,1024]{2,1,0:T(8,128)(2,1)S(1)}, bf16[1,128,1024]{2,1,0:T(8,128)(2,1)}, u32[]{:S(2)}) copy-start(bf16[1,128,1024]{2,1,0:T(8,128)(2,1)} %param.15) | copy-start | bytes 786436
  133.1 99.4 %collective-permute-start = (bf16[64,2048]{1,0:T(8,128)(2,1)S(1)}, bf16[64,2048]{1,0:T(8,128)(2,1)S(1)}, u32[]{:S(2)}, u32[]{:S(2)}) collective-permute-start(bf16[64,2048]{1,0:T(8,128)(2,1)S(1)} %get-tuple-element.43), channel_id=1, source_target_pairs={{0,1},{1,2},{2,3},{3,4},{4,5},{5,6},{6,7},{8,9},{9,10},{10,11},{11... | collective-permute-start | bytes 786440 | tf_op jit(solution)/shard_map/ppermute | solution.py:24
  135.1 97.4 %collective-permute-start.1 = (bf16[64,2048]{1,0:T(8,128)(2,1)S(1)}, bf16[64,2048]{1,0:T(8,128)(2,1)S(1)}, u32[]{:S(2)}, u32[]{:S(2)}) collective-permute-start(bf16[64,2048]{1,0:T(8,128)(2,1)S(1)} %get-tuple-element.44), channel_id=1, source_target_pairs={{1,0},{2,1},{3,2},{4,3},{5,4},{6,5},{7,6},{9,8},{10,9},{11,10},{12... | collective-permute-start | bytes 786440 | tf_op jit(solution)/shard_map/ppermute | solution.py:26
  232.9 1.8 copy-start.12
  236.3 1.0 copy-start.7
  460.9 6.0 copy-start.15
  460.9 17.7 %slice-start = ((s8[10747904]{0:T(1024)(128)(4,1)}), s8[2359296]{0:T(1024)(128)(4,1)S(1)}, s32[]{:S(2)}) async-start(s8[10747904]{0:T(1024)(128)(4,1)} %bitcast.199), calls=%async_computation.6 | async-start | bytes 4718592
  466.9 10.4 copy-start
  466.9 7.5 copy-start.5
  467.0 11.6 %slice-start.1 = ((s8[10747904]{0:T(1024)(128)(4,1)}), s8[4194304]{0:T(1024)(128)(4,1)S(1)}, s32[]{:S(2)}) async-start(s8[10747904]{0:T(1024)(128)(4,1)} %bitcast.199), calls=%async_computation.7 | async-start | bytes 8388608
  467.0 11.6 %slice-start.2 = ((s8[10747904]{0:T(1024)(128)(4,1)}), s8[4194304]{0:T(1024)(128)(4,1)S(1)}, s32[]{:S(2)}) async-start(s8[10747904]{0:T(1024)(128)(4,1)} %bitcast.199), calls=%async_computation.8 | async-start | bytes 8388608
  477.3 1.1 copy-start.6
  478.6 1.7 copy-start.2
  480.4 1.2 copy-start.18
  480.7 0.8 copy-start.10
  481.6 2.6 copy-start.9
  493.1 1.0 copy-start.22
  493.1 1.0 copy-start.23
  494.1 1.2 copy-start.8
  495.4 3.6 copy-start.3
  495.7 12.7 %collective-permute-start.2 = (bf16[64,2048]{0,1:T(8,128)(2,1)S(1)}, bf16[64,2048]{0,1:T(8,128)(2,1)S(1)}, u32[]{:S(2)}, u32[]{:S(2)}) collective-permute-start(bf16[64,2048]{0,1:T(8,128)(2,1)S(1)} %get-tuple-element.31), channel_id=1, source_target_pairs={{0,1},{1,2},{2,3},{3,4},{4,5},{5,6},{6,7},{8,9},{9,10},{10,11},{11... | collective-permute-start | bytes 786440 | tf_op jit(solution)/shard_map/ppermute | solution.py:24
  497.8 10.7 collective-permute-start.3
  499.1 8.9 copy-start.13
  509.1 0.7 copy-start.26
  510.5 6.7 slice-start.3
  510.8 6.5 slice-start.4
  519.7 0.8 copy-start.20
  519.7 1.2 copy-start.19
  578.1 1.8 copy-start.1
  579.8 4.7 copy-start.11
  579.8 4.7 copy-start.16
  579.8 4.7 copy-start.21
  1096.7 1.5 slice-start.5
  1098.2 1.4 copy-start.17
Sparse Core Ops, SparseCore 0:
  9.6 118.0 all-gather.4
  129.2 98.0 all-gather.10
  228.9 44.1 all-gather.6
  274.5 186.4 all-gather.8
  578.2 518.4 reduce-scatter.1
where the time goes:
time: 1120 us; the launch traced here: 1110 us
  waiting for transfers between devices  929 us (83%)
  local copies, waits for them, and re-layouts  73.1 us (7%)
  matrix products  61 us (5%)
  between operations  14.4 us (1%)
  blocking collectives  12.6 us (1%)
  other arithmetic  11.5 us (1%)
    reduce_scatter x1, waiting for transfers between devices, local(): lax.psum_scatter(jnp.concatenate([jnp.einsum('td,te->de', a_one, grad_qkv...  511 us
    all_gather x1, waiting for transfers between devices, local(): lax.all_gather(w_in, 'fsdp', axis=0, tiled=True)  185 us
    all_gather x1, waiting for transfers between devices, local(): lax.all_gather(w_qkv, 'fsdp', axis=0, tiled=True)  104 us
    all_gather x1, waiting for transfers between devices, local(): lax.all_gather(w_mlp_out, 'fsdp', axis=1, tiled=True)  91 us
    concatenate x1, local copies, waits for them, and re-layouts, local(): jnp.concatenate([jnp.einsum('td,te->de', a_one, grad_qkv_b, preferred_ele...  57.2 us
    all_gather x1, waiting for transfers between devices, local(): lax.all_gather(w_attn_out, 'fsdp', axis=0, tiled=True)  34.6 us
  transfers between devices with their start and end apart: 9, of which 5 were waited for; matrix products, arithmetic and copies ran while one was open for 3% of the time, Pallas kernels for 0%

commit v1 on v0

--- a/solution.py
+++ b/solution.py
@@ -1,6 +1,10 @@
+import functools
+
 import jax
 import jax.numpy as jnp
 from jax import lax
+from jax.experimental import pallas as pl
+from jax.experimental.pallas import tpu as pltpu
 from jax.sharding import PartitionSpec as P
 
 HEADS = 16
@@ -11,6 +15,400 @@
 norm_eps = 1e-05
 rope_base = 10000.0
 masked_score = -1e30
+MESH = pl.DeviceIdType.MESH
+LANE = 1024
+SUB = 256
+
+
+def up_to(size, unit):
+    return -(-size // unit) * unit
+
+
+def gather_kernel(n, count, *refs):
+    ins, outs = refs[:count], refs[count : 2 * count]
+    z_send, z_recv, one_send, one_recv, two_send, two_recv, core_send, core_recv, own_sem = refs[
+        2 * count :
+    ]
+    me = lax.axis_index("fsdp")
+    spot = lax.axis_index("seq")
+    core = lax.rem(spot, 2)
+    bit_x = lax.rem(spot // 2, 2)
+    bit_y = lax.rem(spot // 4, 2)
+    part = bit_y * 4 + bit_x * 2 + core
+    base = spot - part
+    height = ins[0].shape[0]
+    block = height // 8
+
+    def flip(number, mask):
+        c = number % 2
+        x = (number // 2) % 2
+        y = number // 4
+        c = 1 - c if mask & 1 else c
+        x = 1 - x if mask & 2 else x
+        y = 1 - y if mask & 4 else y
+        return y * 4 + x * 2 + c
+
+    mates = {mask: base + flip(part, mask) for mask in (1, 2, 4)}
+
+    barrier = pltpu.get_barrier_semaphore()
+
+    def greet(target):
+        pl.semaphore_signal(barrier, inc=1, device_id=target, device_id_type=MESH)
+
+    for mask in (1, 2, 4):
+        greet((me, mates[mask]))
+
+    @pl.when(me > 0)
+    def _():
+        greet((me - 1, spot))
+
+    @pl.when(me < n - 1)
+    def _():
+        greet((me + 1, spot))
+
+    peers = 3 + jnp.where(me > 0, 1, 0) + jnp.where(me < n - 1, 1, 0)
+    pl.semaphore_wait(barrier, peers)
+
+    def region(k, origin, mask):
+        start = pl.multiple_of(origin * height + flip(part, mask) * block, block)
+        return outs[k].at[pl.ds(start, block)]
+
+    def remote(src, dst, send, recv, target):
+        return pltpu.make_async_remote_copy(
+            src_ref=src, dst_ref=dst, send_sem=send, recv_sem=recv, device_id=target, device_id_type=MESH
+        )
+
+    def z_copy(way, origin, k, own=False):
+        if own:
+            src = ins[k].at[pl.ds(pl.multiple_of(part * block, block), block)]
+        else:
+            src = region(k, origin, 0)
+        target = me + 1 if way == 0 else me - 1
+        return remote(
+            src, region(k, origin, 0), z_send.at[way, origin, k], z_recv.at[origin, k], (target, spot)
+        )
+
+    def firsts(k):
+        return (2, 4) if k % 2 == 0 else (4, 2)
+
+    def one_copy(origin, k, mask=0):
+        place = region(k, origin, mask)
+        return remote(
+            place, place, one_send.at[origin, k], one_recv.at[origin, k], (me, mates[firsts(k)[0]])
+        )
+
+    def two_copy(origin, k, index, mask):
+        place = region(k, origin, mask)
+        return remote(
+            place,
+            place,
+            two_send.at[origin, k, index],
+            two_recv.at[origin, k, index],
+            (me, mates[firsts(k)[1]]),
+        )
+
+    def core_copy(origin, k, index, mask):
+        place = region(k, origin, mask)
+        return remote(
+            place,
+            place,
+            core_send.at[origin, k, index],
+            core_recv.at[origin, k, index],
+            (me, mates[1]),
+        )
+
+    def can_go(way):
+        return me < n - 1 if way == 0 else me > 0
+
+    def has(way, d):
+        return me >= d if way == 0 else me + d <= n - 1
+
+    for k in range(count):
+        for way in (0, 1):
+
+            @pl.when(can_go(way))
+            def _(k=k, way=way):
+                z_copy(way, me, k, own=True).start()
+
+    def own_copy(k):
+        rows = pl.ds(pl.multiple_of(me * height, height), height)
+        return pltpu.make_async_copy(ins[k], outs[k].at[rows], own_sem.at[k])
+
+    for k in range(count):
+        own_copy(k).start()
+
+    def came(way, d, k):
+        origin = me - d if way == 0 else me + d
+
+        @pl.when(has(way, d))
+        def _():
+            z_copy(way, origin, k).wait_recv()
+
+            @pl.when(can_go(way))
+            def _():
+                z_copy(way, origin, k).start()
+
+            one_copy(origin, k).start()
+            two_copy(origin, k, 0, 0).start()
+            core_copy(origin, k, 0, 0).start()
+
+    def second(way, d, k):
+        origin = me - d if way == 0 else me + d
+        m_one, m_two = firsts(k)
+
+        @pl.when(has(way, d))
+        def _():
+            one_copy(origin, k, m_one).wait_recv()
+            two_copy(origin, k, 1, m_one).start()
+            core_copy(origin, k, 1, m_one).start()
+
+    def third(way, d, k):
+        origin = me - d if way == 0 else me + d
+        m_one, m_two = firsts(k)
+
+        @pl.when(has(way, d))
+        def _():
+            two_copy(origin, k, 0, m_two).wait_recv()
+            core_copy(origin, k, 2, m_two).start()
+            two_copy(origin, k, 1, m_one + m_two).wait_recv()
+            core_copy(origin, k, 3, m_one + m_two).start()
+
+    def last(way, d, k):
+        origin = me - d if way == 0 else me + d
+        m_one, m_two = firsts(k)
+        masks = (0, m_one, m_two, m_one + m_two)
+
+        @pl.when(has(way, d))
+        def _():
+            for index, mask in enumerate(masks):
+                core_copy(origin, k, index, mask + 1).wait_recv()
+                core_copy(origin, k, index, mask).wait_send()
+            one_copy(origin, k).wait_send()
+            two_copy(origin, k, 0, 0).wait_send()
+            two_copy(origin, k, 1, m_one).wait_send()
+
+            @pl.when(can_go(way))
+            def _():
+                z_copy(way, origin, k).wait_send()
+
+    steps = [(way, d, k) for d in range(1, n) for k in range(count) for way in (0, 1)]
+    lag = 4
+    total = len(steps)
+    for i in range(total + 2 * lag):
+        if i < total:
+            came(*steps[i])
+        if 0 <= i - lag < total:
+            second(*steps[i - lag])
+        if 0 <= i - 2 * lag < total:
+            third(*steps[i - 2 * lag])
+    for step in steps:
+        last(*step)
+    for k in range(count):
+        for way in (0, 1):
+
+            @pl.when(can_go(way))
+            def _(k=k, way=way):
+                z_copy(way, me, k, own=True).wait_send()
+
+        own_copy(k).wait()
+
+
+def gather_weights(shards):
+    n = lax.axis_size("fsdp")
+    count = len(shards)
+    sem = pltpu.SemaphoreType.DMA
+    return pl.pallas_call(
+        functools.partial(gather_kernel, n, count),
+        out_shape=[jax.ShapeDtypeStruct((n * s.shape[0], s.shape[1]), s.dtype) for s in shards],
+        in_specs=[pl.BlockSpec(memory_space=pl.ANY)] * count,
+        out_specs=[pl.BlockSpec(memory_space=pl.ANY)] * count,
+        scratch_shapes=[
+            sem((2, n, count)),
+            sem((n, count)),
+            sem((n, count)),
+            sem((n, count)),
+            sem((n, count, 2)),
+            sem((n, count, 2)),
+            sem((n, count, 4)),
+            sem((n, count, 4)),
+            sem((count,)),
+        ],
+        compiler_params=pltpu.CompilerParams(collective_id=0, has_side_effects=True),
+        name="gather_weights",
+    )(*shards)
+
+
+def scatter_kernel(
+    n, edges, at_ref, b_ref, gcol_ref, out_ref,
+    gbuf, r_core, r_one, r_two, r_z,
+    core_send, core_recv, one_send, one_recv, two_send, two_recv, z_send, z_recv,
+):
+    me = lax.axis_index("fsdp")
+    spot = lax.axis_index("seq")
+    c = lax.rem(spot, 2)
+    x = lax.rem(spot // 2, 2)
+    y = spot // 4
+    r = gbuf.shape[5]
+    chunks = gbuf.shape[0]
+    units = chunks // 2
+    mate_c = y * 4 + x * 2 + (1 - c)
+    mate_x = y * 4 + (1 - x) * 2 + c
+    mate_y = (1 - y) * 4 + x * 2 + c
+
+    barrier = pltpu.get_barrier_semaphore()
+    for mate in (mate_c, mate_x, mate_y):
+        pl.semaphore_signal(barrier, inc=1, device_id=(me, mate), device_id_type=MESH)
+    for d in range(1, n):
+        pl.semaphore_signal(
+            barrier, inc=1, device_id=(lax.rem(me + d, n), spot), device_id_type=MESH
+        )
+    pl.semaphore_wait(barrier, 3 + n - 1)
+
+    def remote(src, dst, send, recv, target):
+        return pltpu.make_async_remote_copy(
+            src_ref=src, dst_ref=dst, send_sem=send, recv_sem=recv, device_id=target, device_id_type=MESH
+        )
+
+    def core_copy(j):
+        return remote(
+            gbuf.at[j, :, :, :, 1 - c], r_core.at[j], core_send.at[j], core_recv.at[j], (me, mate_c)
+        )
+
+    def one_copy(j, e):
+        src = gbuf.at[j, :, :, 1 - x, c] if e == 0 else gbuf.at[j, :, 1 - y, :, c]
+        mate = mate_x if e == 0 else mate_y
+        return remote(src, r_one.at[j], one_send.at[j], one_recv.at[j], (me, mate))
+
+    def two_copy(j, e):
+        src = gbuf.at[j, :, 1 - y, x, c] if e == 0 else gbuf.at[j, :, y, 1 - x, c]
+        mate = mate_y if e == 0 else mate_x
+        return remote(src, r_two.at[j], two_send.at[j], two_recv.at[j], (me, mate))
+
+    def z_copy(j, d):
+        other = lax.rem(me + d, n)
+        return remote(
+            gbuf.at[j, other, y, x, c],
+            r_z.at[j, d - 1],
+            z_send.at[j, d - 1],
+            z_recv.at[j, d - 1],
+            (other, spot),
+        )
+
+    def plus(left, right):
+        return (left.astype(jnp.float32) + right.astype(jnp.float32)).astype(left.dtype)
+
+    def make(k):
+        def one_tile(u, carry):
+            t = k * (2 * LANE // SUB) + u
+            which = jnp.int32(0)
+            for edge in edges:
+                which = which + jnp.where(t >= edge, 1, 0).astype(jnp.int32)
+            columns = pl.ds(pl.multiple_of(t * SUB, SUB), SUB)
+            value = jnp.dot(at_ref[which], b_ref[:, columns], preferred_element_type=jnp.float32)
+            value = value.astype(gbuf.dtype).reshape(gbuf.shape[1:6] + (SUB,))
+            j = k * 2 + u // (LANE // SUB)
+            inner = pl.ds(pl.multiple_of((u % (LANE // SUB)) * SUB, SUB), SUB)
+            gbuf[j, :, :, :, :, :, inner] = value
+            return carry
+
+        lax.fori_loop(0, 2 * LANE // SUB, one_tile, 0)
+
+    def turn(it, carry):
+        @pl.when(it < units)
+        def _():
+            make(it)
+
+            @pl.when(it == units - 1)
+            def _():
+                wide = gcol_ref.shape[1]
+                gbuf[chunks - 1, :, :, :, :, :, LANE - wide :] = gcol_ref[...].reshape(
+                    gbuf.shape[1:6] + (wide,)
+                )
+
+            core_copy(2 * it).start()
+            core_copy(2 * it + 1).start()
+
+        @pl.when((it >= 1) & (it < units + 1))
+        def _():
+            for e in (0, 1):
+                j = 2 * (it - 1) + e
+                core_copy(j).wait()
+                for i in range(n):
+                    for a in (0, 1):
+                        gbuf[j, i, a, :, c] = plus(gbuf[j, i, a, :, c], r_core[j, i, a])
+                one_copy(j, e).start()
+
+        @pl.when((it >= 2) & (it < units + 2))
+        def _():
+            for e in (0, 1):
+                j = 2 * (it - 2) + e
+                one_copy(j, e).wait()
+                for i in range(n):
+                    if e == 0:
+                        gbuf[j, i, :, x, c] = plus(gbuf[j, i, :, x, c], r_one[j, i])
+                    else:
+                        gbuf[j, i, y, :, c] = plus(gbuf[j, i, y, :, c], r_one[j, i])
+                two_copy(j, e).start()
+
+        @pl.when((it >= 3) & (it < units + 3))
+        def _():
+            for e in (0, 1):
+                j = 2 * (it - 3) + e
+                two_copy(j, e).wait()
+                for i in range(n):
+                    gbuf[j, i, y, x, c] = plus(gbuf[j, i, y, x, c], r_two[j, i])
+                for d in range(1, n):
+                    z_copy(j, d).start()
+
+        @pl.when(it >= 4)
+        def _():
+            for e in (0, 1):
+                j = 2 * (it - 4) + e
+                total = gbuf[j, me, y, x, c].astype(jnp.float32)
+                for d in range(1, n):
+                    z_copy(j, d).wait()
+                    total = total + r_z[j, d - 1].astype(jnp.float32)
+                out_ref[:, pl.ds(pl.multiple_of(j * LANE, LANE), LANE)] = total
+
+        return carry
+
+    lax.fori_loop(0, units + 4, turn, 0)
+
+
+def scatter_sums(lefts, rights, gain_columns, edges):
+    n = lax.axis_size("fsdp")
+    rows = lefts.shape[1]
+    r = rows // (8 * n)
+    width = rights.shape[1]
+    chunks = width // LANE
+    half = jnp.bfloat16
+    sem = pltpu.SemaphoreType.DMA
+    vmem = pl.BlockSpec(memory_space=pltpu.VMEM)
+    return pl.pallas_call(
+        functools.partial(scatter_kernel, n, edges),
+        out_shape=jax.ShapeDtypeStruct((r, width), jnp.float32),
+        in_specs=[vmem] * 3,
+        out_specs=vmem,
+        scratch_shapes=[
+            pltpu.VMEM((chunks, n, 2, 2, 2, r, LANE), half),
+            pltpu.VMEM((chunks, n, 2, 2, r, LANE), half),
+            pltpu.VMEM((chunks, n, 2, r, LANE), half),
+            pltpu.VMEM((chunks, n, r, LANE), half),
+            pltpu.VMEM((chunks, n - 1, r, LANE), half),
+            sem((chunks,)),
+            sem((chunks,)),
+            sem((chunks,)),
+            sem((chunks,)),
+            sem((chunks,)),
+            sem((chunks,)),
+            sem((chunks, n - 1)),
+            sem((chunks, n - 1)),
+        ],
+        compiler_params=pltpu.CompilerParams(
+            collective_id=1, has_side_effects=True, vmem_limit_bytes=62 * 1024 * 1024
+        ),
+        name="scatter_sums",
+    )(lefts, rights, gain_columns)
 
 
 def padded(cells, sides, width):
@@ -58,8 +456,8 @@
     return turned.reshape(tok_rows, -1)
 
 
-def gated_gelu(upward):
-    return jax.nn.gelu(upward[:, 0], approximate=False) * upward[:, 1]
+def gated_gelu(gate, linear):
+    return jax.nn.gelu(gate, approximate=False) * linear
 
 
 def local(tokens, segment_ids, w_qkv, w_attn_out, w_in, w_mlp_out, norm_gains, cotangent):
@@ -68,14 +466,27 @@
     half_win = WIN // 2
     score_scale = HD ** (-0.5)
     row_start = lax.axis_index("seq") * tok_rows
-    full_qkv, full_out, full_in, full_mlp, full_gains = (
-        lax.all_gather(w_qkv, "fsdp", axis=0, tiled=True),
-        lax.all_gather(w_attn_out, "fsdp", axis=0, tiled=True),
-        lax.all_gather(w_in, "fsdp", axis=0, tiled=True),
-        lax.all_gather(w_mlp_out, "fsdp", axis=1, tiled=True),
-        lax.all_gather(norm_gains, "fsdp", axis=1, tiled=True),
-    )
-    gain_pair = full_gains.astype(jnp.float32)
+    ff = w_in.shape[2]
+    ff_wide = up_to(ff, 128)
+    tail = up_to(ff_wide + 128, SUB) - ff_wide
+    stretch = ((0, 0), (0, ff_wide - ff))
+    full_qkv, full_out, full_gate, full_lin, full_down = gather_weights(
+        [
+            w_qkv,
+            w_attn_out,
+            jnp.pad(w_in[:, 0], stretch),
+            jnp.pad(w_in[:, 1], stretch),
+            jnp.concatenate(
+                [
+                    jnp.pad(w_mlp_out.T, stretch),
+                    jnp.pad(norm_gains.T, ((0, 0), (0, tail - norm_gains.shape[0]))),
+                ],
+                axis=1,
+            ),
+        ]
+    )
+    full_mlp = full_down[:, :ff_wide]
+    gain_pair = full_down[:, ff_wide : ff_wide + norm_gains.shape[0]].T.astype(jnp.float32)
     inputs = tokens[0].astype(jnp.float32)
     cos_table, sin_table = rope_tables(row_start + jnp.arange(tok_rows, dtype=jnp.int32), HD)
     h_one, norm_one_back = jax.vjp(layer_norm, inputs, gain_pair[0])
@@ -113,18 +524,23 @@
     residual = inputs + jnp.dot(attn_ob, full_out, preferred_element_type=jnp.float32)
     h_two, norm_two_back = jax.vjp(layer_norm, residual, gain_pair[1])
     a_two = h_two.astype(jnp.bfloat16)
-    upward = jnp.einsum("td,dcf->tcf", a_two, full_in, preferred_element_type=jnp.float32)
-    middle, gelu_back = jax.vjp(gated_gelu, upward)
+    gate = jnp.dot(a_two, full_gate, preferred_element_type=jnp.float32)
+    linear = jnp.dot(a_two, full_lin, preferred_element_type=jnp.float32)
+    middle, gelu_back = jax.vjp(gated_gelu, gate, linear)
     middle_b = middle.astype(jnp.bfloat16)
-    outputs = (residual + jnp.dot(middle_b, full_mlp, preferred_element_type=jnp.float32)).astype(
+    outputs = (
+        residual + jnp.einsum("tf,df->td", middle_b, full_mlp, preferred_element_type=jnp.float32)
+    ).astype(
         jnp.bfloat16
     )
-    back_qkv, back_out, back_in, back_mlp = (full_qkv, full_out, full_in, full_mlp)
+    back_qkv, back_out = (full_qkv, full_out)
     grad_out = cotangent[0].astype(jnp.float32)
     grad_mlp_b = grad_out.astype(jnp.bfloat16)
-    grad_mid = jnp.einsum("td,fd->tf", grad_mlp_b, back_mlp, preferred_element_type=jnp.float32)
-    grad_up_b = gelu_back(grad_mid)[0].astype(jnp.bfloat16)
-    grad_a_two = jnp.einsum("tcf,dcf->td", grad_up_b, back_in, preferred_element_type=jnp.float32)
+    grad_mid = jnp.dot(grad_mlp_b, full_mlp, preferred_element_type=jnp.float32)
+    grad_gate_b, grad_lin_b = [g.astype(jnp.bfloat16) for g in gelu_back(grad_mid)]
+    grad_a_two = jnp.einsum(
+        "tf,df->td", grad_gate_b, full_gate, preferred_element_type=jnp.float32
+    ) + jnp.einsum("tf,df->td", grad_lin_b, full_lin, preferred_element_type=jnp.float32)
     grad_res_norm, grad_gain_two = norm_two_back(grad_a_two)
     grad_res = grad_out + grad_res_norm
     grad_att_b = grad_res.astype(jnp.bfloat16)
@@ -178,33 +594,57 @@
     grad_in_norm, grad_gain_one = norm_one_back(grad_a_one)
     input_grad = grad_res + grad_in_norm
     gains_cols = jnp.stack([grad_gain_one, grad_gain_two], axis=1)
-    grad_up_flat = grad_up_b.reshape(tok_rows, -1)
-    ff_width = grad_mid.shape[1]
-    summed = lax.psum_scatter(
-        jnp.concatenate(
-            [
-                jnp.einsum("td,te->de", a_one, grad_qkv_b, preferred_element_type=jnp.float32),
-                jnp.einsum("td,te->de", attn_ob, grad_att_b, preferred_element_type=jnp.float32),
-                jnp.einsum("td,te->de", a_two, grad_up_flat, preferred_element_type=jnp.float32),
-                jnp.einsum("td,tf->df", grad_mlp_b, middle_b, preferred_element_type=jnp.float32),
-                gains_cols,
-            ],
-            axis=1,
-        ),
-        ("fsdp", "seq"),
-        scatter_dimension=0,
-        tiled=True,
-    )
-    own_rows = summed.shape[0]
-    edge_one = 3 * model_width
-    edge_two = edge_one + model_width
-    edge_three = edge_two + 2 * ff_width
-    edge_four = edge_three + ff_width
+    shares = lax.axis_size("fsdp") * lax.axis_size("seq")
+    lefts = [a_one, attn_ob, a_two, grad_mlp_b]
+    widths = [3 * model_width, model_width, 2 * ff_wide, ff_wide]
+    rights = [
+        grad_qkv_b,
+        grad_att_b,
+        jnp.concatenate([grad_gate_b, grad_lin_b], axis=1),
+        middle_b,
+    ]
+    total_width = sum(widths) + tail
+    fits = (
+        lax.axis_size("seq") == 8
+        and model_width % (16 * shares) == 0
+        and total_width % (2 * LANE) == 0
+        and all(w % SUB == 0 for w in widths[:3])
+    )
+    if fits:
+        edges = [sum(widths[: i + 1]) // SUB for i in range(3)]
+        summed = scatter_sums(
+            jnp.stack([left.T for left in lefts]),
+            jnp.concatenate(rights + [jnp.zeros((tok_rows, tail), jnp.bfloat16)], axis=1),
+            jnp.pad(gains_cols, ((0, 0), (0, 128 - gains_cols.shape[1]))).astype(jnp.bfloat16),
+            edges,
+        )
+        gains_at = total_width - 128
+    else:
+        summed = lax.psum_scatter(
+            jnp.concatenate(
+                [
+                    jnp.einsum("td,te->de", left, right, preferred_element_type=jnp.float32)
+                    for left, right in zip(lefts, rights)
+                ]
+                + [gains_cols],
+                axis=1,
+            ),
+            ("fsdp", "seq"),
+            scatter_dimension=0,
+            tiled=True,
+        )
+        gains_at = sum(widths)
+    edge_one = widths[0]
+    edge_two = edge_one + widths[1]
+    edge_three = edge_two + widths[2]
     sum_qkv = summed[:, :edge_one]
     sum_out = summed[:, edge_one:edge_two]
-    sum_in = summed[:, edge_two:edge_three].reshape(own_rows, 2, ff_width)
-    sum_mlp = summed[:, edge_three:edge_four].T
-    sum_gains = summed[:, edge_four:].T
+    sum_in = jnp.stack(
+        [summed[:, edge_two : edge_two + ff], summed[:, edge_two + ff_wide : edge_two + ff_wide + ff]],
+        axis=1,
+    )
+    sum_mlp = summed[:, edge_three : edge_three + ff].T
+    sum_gains = summed[:, gains_at : gains_at + 2].T
     return (outputs[None], input_grad[None], sum_qkv, sum_out, sum_in, sum_mlp, sum_gains)
 
 

time: 1120 us -> 454 us (0.41)
  waiting for transfers between devices: 929 us -> 1.12 us
  Pallas kernels: 0 us -> 341 us
  local copies, waits for them, and re-layouts: 73.1 us -> 40.8 us
  matrix products: 61 us -> 41.9 us
  between operations: 14.4 us -> 1.48 us
  blocking collectives: 12.6 us -> 0 us
    reduce_scatter x1 -> x0, waiting for transfers between devices: 511 us -> none  [local(): lax.psum_scatter(jnp.concatenate([jnp.einsum('td,te->de', a_one, grad_qkv...]
    all_gather x4 -> x0, waiting for transfers between devices: 415 us -> none  [the longest x1 185 us: local(): lax.all_gather(w_in, 'fsdp', axis=0, tiled=True)]
    pallas_call x0 -> x2, Pallas kernels: none -> 341 us  [the longest x1 198 us: gather_weights(): pl.pallas_call(functools.partial(gather_kernel, n, count), out_shape=[jax...]
    concatenate x1, local copies, waits for them, and re-layouts: 57.2 us -> 0.62 us  [local(): jnp.concatenate(rights + [jnp.zeros((tok_rows, tail), jnp.bfloat16)], axi...]
    dot_general x8 -> x6, matrix products: 43 us -> 22.3 us  [the longest x1 6.48 us: local(): grad_mid = jnp.dot(grad_mlp_b, full_mlp, preferred_element_type=jnp.float32)]
    all_gather x1 -> x0, blocking collectives: 12.6 us -> none  [local(): lax.all_gather(norm_gains, 'fsdp', axis=1, tiled=True)]
    unnamed x65 -> x100, local copies, waits for them, and re-layouts: 6.55 us -> 17.8 us
  transfers between devices with their start and end apart: 9 -> 4, of which waited for: 5 -> 2; matrix products, arithmetic and copies ran while one was open for 3% -> 0% of each run, Pallas kernels for 0% -> 0%
where the time goes in v1:
time: 454 us; the launch traced here: 453 us
  Pallas kernels  341 us (75%)
  matrix products  41.9 us (9%)
  local copies, waits for them, and re-layouts  40.8 us (9%)
  other arithmetic  14.5 us (3%)
  starting transfers between devices  12 us (3%)
    pallas_call x1, Pallas kernels, gather_weights(): pl.pallas_call(functools.partial(gather_kernel, n, count), out_shape=[jax...  198 us
    pallas_call x1, Pallas kernels, scatter_sums(): pl.pallas_call(functools.partial(scatter_kernel, n, edges), out_shape=jax...  143 us
    unnamed x100, local copies, waits for them, and re-layouts  17.8 us
    ppermute x2, starting transfers between devices, padded(): lax.ppermute(tail, axis, [(i, (i + 1) % count) for i in range(ends)])  9.27 us
  transfers between devices with their start and end apart: 4, of which 2 were waited for; matrix products, arithmetic and copies ran while one was open for 0% of the time, Pallas kernels for 0%

profile of v1, /device:TPU:0, one launch (start us, length us, event | category | flops | bytes accessed | tf_op | source)
XLA Modules:
  0.0 452.7 jit_solution(13181679597129084866)
XLA Ops:
  0.7 3.0 fusion.64
  3.6 0.9 copy.89
  4.6 1.8 copy.90
  6.4 1.2 pad.31.refs_2_
  7.6 1.2 pad.32.refs_3_
  8.9 1.8 copy.67
  10.7 1.2 fusion.11.refs_4_
  12.0 197.8 %gather_weights.1 = (bf16[1024,3072]{1,0:T(8,128)(2,1)}, bf16[1024,1024]{1,0:T(8,128)(2,1)}, bf16[1024,2688]{1,0:T(8,128)(2,1)}, bf16[1024,2688]{1,0:T(8,128)(2,1)}, bf16[1024,2816]{1,0:T(8,128)(2,1)}) custom-call(bf16[256,3072]{1,0:T(8,128)(2,1)} %refs_0_.1, bf16[256,1024]{1,0:T(8,128)(2,1)} %refs_1_.1, bf16[256,2688]{1,0:T(8,128)(2,1)} %pad.31.refs_2_, ...), custom_call_target="tpu_custom_call" | custom-call | tf_op jit(solution)/shard_map/gather_weights/pallas_call | solution.py:220
  209.8 1.0 convert_bitcast_fusion.1
  211.7 3.8 fusion.59
  217.7 1.3 collective-permute-start.1
  219.0 3.2 collective-permute-start
  223.3 0.9 fusion.67
  225.8 1.5 divide_convert_fusion
  227.6 1.7 convolution_convert_fusion.1
  229.3 0.8 copy.81
  230.1 2.2 fusion.69
  232.6 0.8 fusion.98
  233.5 3.7 fusion.70
  237.2 6.5 %multiply_convert_fusion.1 = (bf16[128,2688]{1,0:T(8,128)(2,1)S(1)}, f32[128,2688]{1,0:T(8,128)S(1)}, f32[128,2688]{1,0:T(8,128)S(1)}) fusion(f32[128,2688]{1,0:T(8,128)S(1)} %fusion.70, bf16[1024,2816]{1,0:T(8,128)(2,1)} %get-tuple-element.12, bf16[1,128,1024]{2,1,0:T(8,128)(2,1)S(1)} %copy-done.20), kind=kOutput, calls=%fused_computation.23 | convolution fusion | flops 727351296 | bytes 10584064 | tf_op jit(solution)/shard_map/dot_general | solution.py:539
  243.7 2.6 add_convert_fusion
  246.3 1.9 fusion.71
  248.2 2.6 multiply_reduce_fusion.1
  251.1 0.8 copy-done.9
  252.7 1.5 convolution_convert_fusion
  254.2 1.8 copy.75
  256.0 2.7 fusion.72
  258.7 1.1 multiply_reduce_fusion
  262.0 1.6 copy.77
  263.8 1.4 collective-permute-start.3
  265.2 6.0 %collective-permute-start.2 = (bf16[64,2048]{1,0:T(8,128)(2,1)S(1)}, bf16[64,2048]{1,0:T(8,128)(2,1)S(1)}, u32[]{:S(2)}, u32[]{:S(2)}) collective-permute-start(bf16[64,2048]{1,0:T(8,128)(2,1)S(1)} %get-tuple-element.59), channel_id=1, source_target_pairs={{0,1},{1,2},{2,3},{3,4},{4,5},{5,6},{6,7},{8,9},{9,10},{10,11},{11... | collective-permute-start | bytes 786440 | tf_op jit(solution)/shard_map/ppermute | solution.py:422
  273.3 1.0 copy-done.13
  275.4 0.8 constant_dynamic-update-slice_fusion.7
  277.1 1.9 constant_dynamic-update-slice_fusion.5
  279.7 0.9 constant_dynamic-update-slice_fusion.3
  280.7 0.9 constant_dynamic-update-slice_fusion.2
  281.6 5.1 %fusion.47 = (f32[128]{0:T(128)S(1)}, f32[128,1024]{1,0:T(8,128)S(1)}) fusion(bf16[1,128,1024]{2,1,0:T(8,128)(2,1)S(1)} %copy-done.2, f32[1024]{0:T(1024)S(1)} %get-tuple-element.43, f32[128]{0:T(128)S(1)} %copy-done.31, bf16[1024,3072]{1,0:T(8,128)(2,1)} %get-tuple-element.13, bf16[128,1024]{1,0:T(8,128)(2,1)S(1)} %get-tuple-element.47, ...), kind=kOutput, calls=%fused_computation.78 | convolution fusion | flops 808320896 | bytes 7869440 | tf_op jit(solution)/shard_map/te,de->td/dot_general | solution.py:593
  287.2 1.1 fusion.58
  288.3 1.1 pad_maximum_fusion.2
  289.5 2.4 copy.85.at_ref
  291.8 2.8 constant_dynamic-update-slice_fusion.1
  295.5 0.8 pad.38.gcol_ref
  296.3 143.2 %scatter_sums.1 = f32[32,12288]{1,0:T(8,128)} custom-call(bf16[4,1024,128]{2,1,0:T(8,128)(2,1)} %copy.85.at_ref, bf16[128,12288]{1,0:T(8,128)(2,1)} %constant_dynamic-update-slice_fusion.b_ref, bf16[1024,128]{1,0:T(8,128)(2,1)} %pad.38.gcol_ref), custom_call_target="tpu_custom_call" | custom-call | tf_op jit(solution)/shard_map/scatter_sums/pallas_call | solution.py:387
  439.4 1.8 slice.137
  441.2 1.6 slice.138
  442.8 2.0 slice_bitcast_fusion
  445.5 5.1 %fusion.25 = bf16[1,128,1024]{2,1,0:T(8,128)(2,1)} fusion(f32[128,1024]{1,0:T(8,128)S(1)} %get-tuple-element.85, bf16[128,2688]{1,0:T(8,128)(2,1)S(1)} %get-tuple-element.45, bf16[1024,2816]{1,0:T(8,128)(2,1)} %get-tuple-element.12), kind=kOutput, calls=%fused_computation.49 | convolution fusion | flops 704905216 | bytes 6979584 | tf_op jit(solution)/shard_map/tf,df->td/dot_general | solution.py:532
  450.7 1.4 copy.86
  (153 shorter events, 16.9 us)
Async XLA Ops:
  7.6 1.2 copy-start.36
  209.8 1.5 copy-start.2
  211.5 4.1 copy-start.30
  211.7 3.9 copy-start.37
  211.7 3.9 copy-start.32
  216.9 0.6 copy-start.27
  217.0 7.3 %copy-start.23 = (bf16[128,16,32]{0,2,1:T(8,128)(2,1)}, bf16[128,16,32]{0,2,1:T(8,128)(2,1)S(1)}, u32[]{:S(2)}) copy-start(bf16[128,16,32]{0,2,1:T(8,128)(2,1)S(1)} %get-tuple-element.68) | copy-start | bytes 393220
  217.1 5.2 %copy-start.35 = (s32[1,1024]{1,0:T(1,128)S(1)}, s32[1,1024]{1,0:T(1,128)}, u32[]{:S(2)}) copy-start(s32[1,1024]{1,0:T(1,128)} %param.9) | copy-start | bytes 12292
  217.7 4.7 %collective-permute-start.1 = (bf16[64,2048]{1,0:T(8,128)(2,1)S(1)}, bf16[64,2048]{1,0:T(8,128)(2,1)S(1)}, u32[]{:S(2)}, u32[]{:S(2)}) collective-permute-start(bf16[64,2048]{1,0:T(8,128)(2,1)S(1)} %get-tuple-element.72), channel_id=1, source_target_pairs={{1,0},{2,1},{3,2},{4,3},{5,4},{6,5},{7,6},{9,8},{10,9},{11,10},{12... | collective-permute-start | bytes 786440 | tf_op jit(solution)/shard_map/ppermute | solution.py:424
  219.0 4.2 collective-permute-start
  224.4 0.8 copy-start.11
  225.8 1.5 copy-start.22
  229.3 0.9 copy-start.19
  232.4 4.8 %copy-start.20 = (bf16[1,128,1024]{2,1,0:T(8,128)(2,1)S(1)}, bf16[1,128,1024]{2,1,0:T(8,128)(2,1)}, u32[]{:S(2)}) copy-start(bf16[1,128,1024]{2,1,0:T(8,128)(2,1)} %param.15) | copy-start | bytes 786436
  233.5 10.3 %slice-start = ((s8[5505024]{0:T(1024)(128)(4,1)}), s8[4194304]{0:T(1024)(128)(4,1)S(1)}, s32[]{:S(2)}) async-start(s8[5505024]{0:T(1024)(128)(4,1)} %bitcast.125), calls=%async_computation | async-start | bytes 8388608
  233.5 12.9 %slice-start.2 = ((s8[5505024]{0:T(1024)(128)(4,1)}), s8[4194304]{0:T(1024)(128)(4,1)S(1)}, s32[]{:S(2)}) async-start(s8[5505024]{0:T(1024)(128)(4,1)} %bitcast.127), calls=%async_computation.2 | async-start | bytes 8388608
  237.2 6.5 %copy-start = (f32[128,2688]{1,0:T(8,128)}, f32[128,2688]{1,0:T(8,128)S(1)}, u32[]{:S(2)}) copy-start(f32[128,2688]{1,0:T(8,128)S(1)} %fusion.70) | copy-start | bytes 4128772
  237.2 6.6 %slice-start.1 = ((s8[5505024]{0:T(1024)(128)(4,1)}), s8[1310720]{0:T(1024)(128)(4,1)S(1)}, s32[]{:S(2)}) async-start(s8[5505024]{0:T(1024)(128)(4,1)} %bitcast.125), calls=%async_computation.1 | async-start | bytes 2621440
  237.2 9.1 %slice-start.3 = ((s8[5505024]{0:T(1024)(128)(4,1)}), s8[1310720]{0:T(1024)(128)(4,1)S(1)}, s32[]{:S(2)}) async-start(s8[5505024]{0:T(1024)(128)(4,1)} %bitcast.127), calls=%async_computation.3 | async-start | bytes 2621440
  243.7 2.6 copy-start.8
  243.7 4.5 %copy-start.14 = (bf16[128,2688]{1,0:T(8,128)(2,1)}, bf16[128,2688]{1,0:T(8,128)(2,1)S(1)}, u32[]{:S(2)}) copy-start(bf16[128,2688]{1,0:T(8,128)(2,1)S(1)} %get-tuple-element.50) | copy-start | bytes 2064388
  246.3 1.9 copy-start.6
  250.8 1.9 copy-start.5
  251.1 0.8 copy-start.9
  252.0 0.7 copy-start.17
  256.0 2.7 copy-start.16
  259.8 0.9 copy-start.24
  260.7 1.0 copy-start.3
  263.6 7.7 %copy-start.34 = (bf16[1024]{0:T(1024)(128)(2,1)S(1)}, bf16[1024]{0:T(1024)(128)(2,1)}, u32[]{:S(2)}) copy-start(bf16[1024]{0:T(1024)(128)(2,1)} %get-tuple-element.38) | copy-start | bytes 6148
  263.6 7.7 %copy-start.4 = (bf16[16,128,256]{2,1,0:T(8,128)(2,1)S(1)}, bf16[16,128,256]{2,1,0:T(8,128)(2,1)}, u32[]{:S(2)}) copy-start(bf16[16,128,256]{2,1,0:T(8,128)(2,1)} %copy-done.3) | copy-start | bytes 3145732
  263.6 7.7 %copy-start.12 = (bf16[256,1024]{0,1:T(8,128)(2,1)S(1)}, bf16[256,1024]{0,1:T(8,128)(2,1)}, u32[]{:S(2)}) copy-start(bf16[256,1024]{0,1:T(8,128)(2,1)} %copy-done.11) | copy-start | bytes 1572868
  263.8 8.0 %collective-permute-start.3 = (bf16[64,2048]{1,0:T(8,128)(2,1)S(1)}, bf16[64,2048]{1,0:T(8,128)(2,1)S(1)}, u32[]{:S(2)}, u32[]{:S(2)}) collective-permute-start(bf16[64,2048]{1,0:T(8,128)(2,1)S(1)} %get-tuple-element.60), channel_id=1, source_target_pairs={{1,0},{2,1},{3,2},{4,3},{5,4},{6,5},{7,6},{9,8},{10,9},{11,10},{12... | collective-permute-start | bytes 786440 | tf_op jit(solution)/shard_map/ppermute | solution.py:424
  265.2 7.0 %collective-permute-start.2 = (bf16[64,2048]{1,0:T(8,128)(2,1)S(1)}, bf16[64,2048]{1,0:T(8,128)(2,1)S(1)}, u32[]{:S(2)}, u32[]{:S(2)}) collective-permute-start(bf16[64,2048]{1,0:T(8,128)(2,1)S(1)} %get-tuple-element.59), channel_id=1, source_target_pairs={{0,1},{1,2},{2,3},{3,4},{4,5},{5,6},{6,7},{8,9},{9,10},{10,11},{11... | collective-permute-start | bytes 786440 | tf_op jit(solution)/shard_map/ppermute | solution.py:422
  272.4 0.7 copy-start.39
  273.3 1.0 copy-start.13
  274.3 0.7 copy-start.28
  274.3 0.7 copy-start.29
  275.3 3.7 copy-start.18
  275.4 4.3 copy-start.7
  277.1 3.6 copy-start.15
  279.7 1.9 copy-start.31
  281.6 5.2 %copy-start.38 = (f32[128]{0:T(128)S(1)}, f32[128]{0:T(128)}, u32[]{:S(2)}) copy-start(f32[128]{0:T(128)} %copy-done.37) | copy-start | bytes 1540
  281.6 5.2 %copy-start.33 = (f32[128]{0:T(128)S(1)}, f32[128]{0:T(128)}, u32[]{:S(2)}) copy-start(f32[128]{0:T(128)} %copy-done.32) | copy-start | bytes 1540
  281.6 5.6 %copy-start.10 = (f32[128,1024]{1,0:T(8,128)S(1)}, f32[128,1024]{1,0:T(8,128)}, u32[]{:S(2)}) copy-start(f32[128,1024]{1,0:T(8,128)} %copy-done.9) | copy-start | bytes 1572868
  281.6 5.6 %copy-start.21 = (bf16[1,128,1024]{2,1,0:T(8,128)(2,1)S(1)}, bf16[1,128,1024]{2,1,0:T(8,128)(2,1)}, u32[]{:S(2)}) copy-start(bf16[1,128,1024]{2,1,0:T(8,128)(2,1)} %param.15) | copy-start | bytes 786436
  286.8 1.5 copy-start.25
  286.8 1.5 copy-start.26
  289.5 2.4 copy-start.1

commit v2 on v1

--- a/solution.py
+++ b/solution.py
@@ -18,6 +18,7 @@
 MESH = pl.DeviceIdType.MESH
 LANE = 1024
 SUB = 256
+LAGS = (6, 12)
 
 
 def up_to(size, unit):
@@ -27,8 +28,9 @@
 def gather_kernel(n, count, *refs):
     ins, outs = refs[:count], refs[count : 2 * count]
     z_send, z_recv, one_send, one_recv, two_send, two_recv, core_send, core_recv, own_sem = refs[
-        2 * count :
+        2 * count : 2 * count + 9
     ]
+    held = refs[2 * count + 9 :]
     me = lax.axis_index("fsdp")
     spot = lax.axis_index("seq")
     core = lax.rem(spot, 2)
@@ -130,12 +132,18 @@
             def _(k=k, way=way):
                 z_copy(way, me, k, own=True).start()
 
-    def own_copy(k):
+    def own_in(k):
+        return pltpu.make_async_copy(ins[k], held[k], own_sem.at[0, k])
+
+    def own_out(k):
         rows = pl.ds(pl.multiple_of(me * height, height), height)
-        return pltpu.make_async_copy(ins[k], outs[k].at[rows], own_sem.at[k])
+        return pltpu.make_async_copy(held[k], outs[k].at[rows], own_sem.at[1, k])
 
     for k in range(count):
-        own_copy(k).start()
+        own_in(k).start()
+    for k in range(count):
+        own_in(k).wait()
+        own_out(k).start()
 
     def came(way, d, k):
         origin = me - d if way == 0 else me + d
@@ -192,15 +200,15 @@
                 z_copy(way, origin, k).wait_send()
 
     steps = [(way, d, k) for d in range(1, n) for k in range(count) for way in (0, 1)]
-    lag = 4
+    lag_one, lag_two = LAGS
     total = len(steps)
-    for i in range(total + 2 * lag):
+    for i in range(total + lag_two):
         if i < total:
             came(*steps[i])
-        if 0 <= i - lag < total:
-            second(*steps[i - lag])
-        if 0 <= i - 2 * lag < total:
-            third(*steps[i - 2 * lag])
+        if 0 <= i - lag_one < total:
+            second(*steps[i - lag_one])
+        if 0 <= i - lag_two < total:
+            third(*steps[i - lag_two])
     for step in steps:
         last(*step)
     for k in range(count):
@@ -210,7 +218,7 @@
             def _(k=k, way=way):
                 z_copy(way, me, k, own=True).wait_send()
 
-        own_copy(k).wait()
+        own_out(k).wait()
 
 
 def gather_weights(shards):
@@ -231,9 +239,12 @@
             sem((n, count, 2)),
             sem((n, count, 4)),
             sem((n, count, 4)),
-            sem((count,)),
-        ],
-        compiler_params=pltpu.CompilerParams(collective_id=0, has_side_effects=True),
+            sem((2, count)),
+        ]
+        + [pltpu.VMEM(s.shape, s.dtype) for s in shards],
+        compiler_params=pltpu.CompilerParams(
+            collective_id=0, has_side_effects=True, vmem_limit_bytes=32 * 1024 * 1024
+        ),
         name="gather_weights",
     )(*shards)
 

time: 454 us -> 369 us (0.81)
  Pallas kernels: 341 us -> 245 us
  local copies, waits for them, and re-layouts: 40.8 us -> 47.7 us
    pallas_call x1, Pallas kernels: 198 us -> 102 us  [gather_weights(): pl.pallas_call(functools.partial(gather_kernel, n, count), out_shape=[jax...]
    unnamed x100 -> x112, local copies, waits for them, and re-layouts: 17.8 us -> 21.8 us
  transfers between devices with their start and end apart: 4 -> 4, of which waited for: 2 -> 1; matrix products, arithmetic and copies ran while one was open for 0% -> 0% of each run, Pallas kernels for 0% -> 0%
where the time goes in v2:
time: 369 us; the launch traced here: 368 us
  Pallas kernels  245 us (66%)
  local copies, waits for them, and re-layouts  47.7 us (13%)
  matrix products  43.8 us (12%)
  other arithmetic  16.9 us (5%)
  starting transfers between devices  12.6 us (3%)
    pallas_call x1, Pallas kernels, scatter_sums(): pl.pallas_call(functools.partial(scatter_kernel, n, edges), out_shape=jax...  143 us
    pallas_call x1, Pallas kernels, gather_weights(): pl.pallas_call(functools.partial(gather_kernel, n, count), out_shape=[jax...  102 us
    unnamed x112, local copies, waits for them, and re-layouts  21.8 us
    ppermute x2, starting transfers between devices, padded(): lax.ppermute(tail, axis, [(i, (i + 1) % count) for i in range(ends)])  9.91 us
  transfers between devices with their start and end apart: 4, of which 1 were waited for; matrix products, arithmetic and copies ran while one was open for 0% of the time, Pallas kernels for 0%

profile of v2, /device:TPU:0, one launch (start us, length us, event | category | flops | bytes accessed | tf_op | source)
XLA Modules:
  0.0 367.6 jit_solution(10684981722242451393)
XLA Ops:
  0.7 3.0 fusion.64
  3.7 1.8 copy.89
  5.4 1.7 copy.90
  7.3 1.2 copy-done.14
  8.5 1.2 pad.32.refs_3_
  9.8 1.8 copy.67
  11.8 1.2 copy-done.2
  13.1 1.4 copy-done.3
  14.5 101.5 %gather_weights.1 = (bf16[1024,3072]{1,0:T(8,128)(2,1)}, bf16[1024,1024]{1,0:T(8,128)(2,1)S(1)}, bf16[1024,2688]{1,0:T(8,128)(2,1)S(1)}, bf16[1024,2688]{1,0:T(8,128)(2,1)S(1)}, bf16[1024,2816]{1,0:T(8,128)(2,1)}) custom-call(bf16[256,3072]{1,0:T(8,128)(2,1)S(1)} %copy-done.3, bf16[256,1024]{1,0:T(8,128)(2,1)S(1)} %copy-done.4, ...), custom_call_target="tpu_custom_call" | custom-call | tf_op jit(solution)/shard_map/gather_weights/pallas_call | solution.py:228
  116.1 1.3 convert_bitcast_fusion.1
  118.3 5.5 %fusion.59 = f32[128,3072]{1,0:T(8,128)S(1)} fusion(bf16[1024,3072]{1,0:T(8,128)(2,1)} %get-tuple-element.13, bf16[1,128,1024]{2,1,0:T(8,128)(2,1)S(1)} %copy-done.9, f32[1024]{0:T(1024)S(1)} %get-tuple-element.43, f32[128]{0:T(128)S(1)} %fusion.53, f32[128]{0:T(128)S(1)} %broadcast_multiply_fusion.1), kind=kOutput, calls=%fused_computation.146 | convolution fusion | flops 805961728 | bytes 8131584 | tf_op jit(solution)/shard_map/dot_general | solution.py:505
  123.8 1.0 fusion.65
  124.9 1.2 copy.72
  126.1 2.0 copy.69
  128.9 1.8 subtract_convert_fusion.2
  131.0 1.3 collective-permute-start.1
  132.3 3.8 %collective-permute-start = (bf16[64,2048]{1,0:T(8,128)(2,1)S(1)}, bf16[64,2048]{1,0:T(8,128)(2,1)}, u32[]{:S(2)}, u32[]{:S(2)}) collective-permute-start(bf16[64,2048]{1,0:T(8,128)(2,1)S(1)} %get-tuple-element.71), channel_id=1, source_target_pairs={{0,1},{1,2},{2,3},{3,4},{4,5},{5,6},{6,7},{8,9},{9,10},{10,11},{11... | collective-permute-start | bytes 786440 | tf_op jit(solution)/shard_map/ppermute | solution.py:433
  136.8 1.1 pad_maximum_fusion.1
  139.0 1.7 fusion.68
  141.4 1.5 divide_convert_fusion
  143.1 1.7 convolution_convert_fusion.1
  145.7 1.5 fusion.69
  148.3 3.7 %fusion.70 = f32[128,2688]{1,0:T(8,128)S(1)} fusion(bf16[1024,2688]{1,0:T(8,128)(2,1)} %copy-done.1, f32[128,1024]{1,0:T(8,128)S(1)} %get-tuple-element.85, f32[1024]{0:T(1024)S(1)} %get-tuple-element.42, f32[128]{0:T(128)S(1)} %fusion.54, f32[128]{0:T(128)S(1)} %broadcast_multiply_fusion), kind=kOutput, calls=%fused_computation.155 | convolution fusion | flops 705167360 | bytes 7410688 | tf_op jit(solution)/shard_map/dot_general | solution.py:538
  152.0 6.5 %multiply_convert_fusion.1 = (bf16[128,2688]{1,0:T(8,128)(2,1)S(1)}, f32[128,2688]{1,0:T(8,128)S(1)}, f32[128,2688]{1,0:T(8,128)S(1)}) fusion(f32[128,2688]{1,0:T(8,128)S(1)} %fusion.70, bf16[1024,2816]{1,0:T(8,128)(2,1)} %get-tuple-element.12, bf16[1,128,1024]{2,1,0:T(8,128)(2,1)S(1)} %copy-done.27), kind=kOutput, calls=%fused_computation.23 | convolution fusion | flops 727351296 | bytes 10584064 | tf_op jit(solution)/shard_map/dot_general | solution.py:550
  158.6 2.6 add_convert_fusion
  161.2 1.9 fusion.71
  163.1 2.6 multiply_reduce_fusion.1
  167.5 1.5 convolution_convert_fusion
  169.1 1.9 copy.75
  171.0 2.6 fusion.72
  173.7 1.1 multiply_reduce_fusion
  177.0 1.6 copy.77
  178.7 1.4 collective-permute-start.3
  180.2 6.2 %collective-permute-start.2 = (bf16[64,2048]{1,0:T(8,128)(2,1)S(1)}, bf16[64,2048]{1,0:T(8,128)(2,1)S(1)}, u32[]{:S(2)}, u32[]{:S(2)}) collective-permute-start(bf16[64,2048]{1,0:T(8,128)(2,1)S(1)} %get-tuple-element.59), channel_id=1, source_target_pairs={{0,1},{1,2},{2,3},{3,4},{4,5},{5,6},{6,7},{8,9},{9,10},{10,11},{11... | collective-permute-start | bytes 786440 | tf_op jit(solution)/shard_map/ppermute | solution.py:433
  188.4 1.0 copy-done.20
  192.1 1.9 constant_dynamic-update-slice_fusion.5
  195.6 0.9 constant_dynamic-update-slice_fusion.2
  196.6 5.1 %fusion.47 = (f32[128]{0:T(128)S(1)}, f32[128,1024]{1,0:T(8,128)S(1)}) fusion(bf16[1,128,1024]{2,1,0:T(8,128)(2,1)S(1)} %copy-done.9, f32[1024]{0:T(1024)S(1)} %get-tuple-element.43, f32[128]{0:T(128)S(1)} %copy-done.37, bf16[1024,3072]{1,0:T(8,128)(2,1)} %get-tuple-element.13, bf16[128,1024]{1,0:T(8,128)(2,1)S(1)} %get-tuple-element.47, ...), kind=kOutput, calls=%fused_computation.78 | convolution fusion | flops 808320896 | bytes 7869440 | tf_op jit(solution)/shard_map/te,de->td/dot_general | solution.py:604
  202.2 1.1 fusion.58
  203.3 1.1 pad_maximum_fusion.2
  204.4 2.4 copy.85.at_ref
  206.8 2.8 constant_dynamic-update-slice_fusion.1
  211.2 143.1 %scatter_sums.1 = f32[32,12288]{1,0:T(8,128)} custom-call(bf16[4,1024,128]{2,1,0:T(8,128)(2,1)} %copy.85.at_ref, bf16[128,12288]{1,0:T(8,128)(2,1)} %constant_dynamic-update-slice_fusion.b_ref, bf16[1024,128]{1,0:T(8,128)(2,1)} %pad.38.gcol_ref), custom_call_target="tpu_custom_call" | custom-call | tf_op jit(solution)/shard_map/scatter_sums/pallas_call | solution.py:398
  354.3 1.8 slice.137
  356.1 1.6 slice.138
  357.7 2.0 slice_bitcast_fusion
  360.4 5.2 %fusion.25 = bf16[1,128,1024]{2,1,0:T(8,128)(2,1)} fusion(f32[128,1024]{1,0:T(8,128)S(1)} %get-tuple-element.85, bf16[128,2688]{1,0:T(8,128)(2,1)S(1)} %get-tuple-element.45, bf16[1024,2816]{1,0:T(8,128)(2,1)} %get-tuple-element.12), kind=kOutput, calls=%fused_computation.49 | convolution fusion | flops 704905216 | bytes 6979584 | tf_op jit(solution)/shard_map/tf,df->td/dot_general | solution.py:543
  365.6 1.4 copy.86
  (165 shorter events, 21.1 us)
Async XLA Ops:
  7.1 1.3 copy-start.14
  7.2 2.4 copy-start.42
  11.6 1.3 copy-start.2
  11.6 1.4 copy-start.4
  13.1 1.4 copy-start.3
  116.1 7.7 %copy-start = (bf16[1024,2688]{1,0:T(8,128)(2,1)}, bf16[1024,2688]{1,0:T(8,128)(2,1)S(1)}, u32[]{:S(2)}) copy-start(bf16[1024,2688]{1,0:T(8,128)(2,1)S(1)} %get-tuple-element.16) | copy-start | bytes 16515076
  116.1 7.7 %copy-start.1 = (bf16[1024,2688]{1,0:T(8,128)(2,1)}, bf16[1024,2688]{1,0:T(8,128)(2,1)S(1)}, u32[]{:S(2)}) copy-start(bf16[1024,2688]{1,0:T(8,128)(2,1)S(1)} %get-tuple-element.15) | copy-start | bytes 16515076
  116.1 1.8 copy-start.9
  118.0 5.8 %copy-start.36 = (f32[128]{0:T(128)}, f32[128]{0:T(128)S(1)}, u32[]{:S(2)}) copy-start(f32[128]{0:T(128)S(1)} %broadcast_multiply_fusion.1) | copy-start | bytes 1540
  118.2 5.6 %copy-start.43 = (f32[128]{0:T(128)}, f32[128]{0:T(128)S(1)}, u32[]{:S(2)}) copy-start(f32[128]{0:T(128)S(1)} %fusion.46) | copy-start | bytes 1540
  118.2 5.6 %copy-start.38 = (f32[128]{0:T(128)}, f32[128]{0:T(128)S(1)}, u32[]{:S(2)}) copy-start(f32[128]{0:T(128)S(1)} %fusion.53) | copy-start | bytes 1540
  128.9 1.9 copy-start.33
  130.8 5.3 %copy-start.41 = (s32[1,1024]{1,0:T(1,128)S(1)}, s32[1,1024]{1,0:T(1,128)}, u32[]{:S(2)}) copy-start(s32[1,1024]{1,0:T(1,128)} %param.9) | copy-start | bytes 12292
  131.0 5.8 %collective-permute-start.1 = (bf16[64,2048]{1,0:T(8,128)(2,1)S(1)}, bf16[64,2048]{1,0:T(8,128)(2,1)}, u32[]{:S(2)}, u32[]{:S(2)}) collective-permute-start(bf16[64,2048]{1,0:T(8,128)(2,1)S(1)} %get-tuple-element.72), channel_id=1, source_target_pairs={{1,0},{2,1},{3,2},{4,3},{5,4},{6,5},{7,6},{9,8},{10,9},{11,10},{12... | collective-permute-start | bytes 786440 | tf_op jit(solution)/shard_map/ppermute | solution.py:435
  132.3 4.6 %collective-permute-start = (bf16[64,2048]{1,0:T(8,128)(2,1)S(1)}, bf16[64,2048]{1,0:T(8,128)(2,1)}, u32[]{:S(2)}, u32[]{:S(2)}) collective-permute-start(bf16[64,2048]{1,0:T(8,128)(2,1)S(1)} %get-tuple-element.71), channel_id=1, source_target_pairs={{0,1},{1,2},{2,3},{3,4},{4,5},{5,6},{6,7},{8,9},{9,10},{10,11},{11... | collective-permute-start | bytes 786440 | tf_op jit(solution)/shard_map/ppermute | solution.py:433
  139.0 1.7 copy-start.18
  140.7 2.2 copy-start.5
  141.4 1.5 copy-start.29
  147.2 4.8 %copy-start.27 = (bf16[1,128,1024]{2,1,0:T(8,128)(2,1)S(1)}, bf16[1,128,1024]{2,1,0:T(8,128)(2,1)}, u32[]{:S(2)}) copy-start(bf16[1,128,1024]{2,1,0:T(8,128)(2,1)} %param.15) | copy-start | bytes 786436
  148.3 10.3 %slice-start = ((s8[5505024]{0:T(1024)(128)(4,1)}), s8[4194304]{0:T(1024)(128)(4,1)S(1)}, s32[]{:S(2)}) async-start(s8[5505024]{0:T(1024)(128)(4,1)} %bitcast.125), calls=%async_computation | async-start | bytes 8388608
  148.3 12.9 %slice-start.2 = ((s8[5505024]{0:T(1024)(128)(4,1)}), s8[4194304]{0:T(1024)(128)(4,1)S(1)}, s32[]{:S(2)}) async-start(s8[5505024]{0:T(1024)(128)(4,1)} %bitcast.127), calls=%async_computation.2 | async-start | bytes 8388608
  152.0 6.5 %copy-start.7 = (f32[128,2688]{1,0:T(8,128)}, f32[128,2688]{1,0:T(8,128)S(1)}, u32[]{:S(2)}) copy-start(f32[128,2688]{1,0:T(8,128)S(1)} %fusion.70) | copy-start | bytes 4128772
  152.0 6.6 %slice-start.1 = ((s8[5505024]{0:T(1024)(128)(4,1)}), s8[1310720]{0:T(1024)(128)(4,1)S(1)}, s32[]{:S(2)}) async-start(s8[5505024]{0:T(1024)(128)(4,1)} %bitcast.125), calls=%async_computation.1 | async-start | bytes 2621440
  152.0 9.1 %slice-start.3 = ((s8[5505024]{0:T(1024)(128)(4,1)}), s8[1310720]{0:T(1024)(128)(4,1)S(1)}, s32[]{:S(2)}) async-start(s8[5505024]{0:T(1024)(128)(4,1)} %bitcast.127), calls=%async_computation.3 | async-start | bytes 2621440
  158.5 2.6 copy-start.15
  158.5 4.5 %copy-start.21 = (bf16[128,2688]{1,0:T(8,128)(2,1)}, bf16[128,2688]{1,0:T(8,128)(2,1)S(1)}, u32[]{:S(2)}) copy-start(bf16[128,2688]{1,0:T(8,128)(2,1)S(1)} %get-tuple-element.50) | copy-start | bytes 2064388
  161.1 1.9 copy-start.12
  169.1 4.6 %copy-start.6 = (f32[16,128,256]{2,1,0:T(8,128)S(1)}, f32[16,128,256]{2,1,0:T(8,128)}, u32[]{:S(2)}) copy-start(f32[16,128,256]{2,1,0:T(8,128)} %copy-done.5) | copy-start | bytes 6291460
  171.0 2.6 copy-start.23
  174.7 0.9 copy-start.30
  175.6 1.0 copy-start.10
  178.5 7.8 %copy-start.40 = (bf16[1024]{0:T(1024)(128)(2,1)S(1)}, bf16[1024]{0:T(1024)(128)(2,1)}, u32[]{:S(2)}) copy-start(bf16[1024]{0:T(1024)(128)(2,1)} %get-tuple-element.38) | copy-start | bytes 6148
  178.5 7.8 %copy-start.11 = (bf16[16,128,256]{2,1,0:T(8,128)(2,1)S(1)}, bf16[16,128,256]{2,1,0:T(8,128)(2,1)}, u32[]{:S(2)}) copy-start(bf16[16,128,256]{2,1,0:T(8,128)(2,1)} %copy-done.10) | copy-start | bytes 3145732
  178.5 7.8 %copy-start.19 = (bf16[256,1024]{0,1:T(8,128)(2,1)S(1)}, bf16[256,1024]{0,1:T(8,128)(2,1)}, u32[]{:S(2)}) copy-start(bf16[256,1024]{0,1:T(8,128)(2,1)} %copy-done.18) | copy-start | bytes 1572868
  178.7 8.1 %collective-permute-start.3 = (bf16[64,2048]{1,0:T(8,128)(2,1)S(1)}, bf16[64,2048]{1,0:T(8,128)(2,1)S(1)}, u32[]{:S(2)}, u32[]{:S(2)}) collective-permute-start(bf16[64,2048]{1,0:T(8,128)(2,1)S(1)} %get-tuple-element.60), channel_id=1, source_target_pairs={{1,0},{2,1},{3,2},{4,3},{5,4},{6,5},{7,6},{9,8},{10,9},{11,10},{12... | collective-permute-start | bytes 786440 | tf_op jit(solution)/shard_map/ppermute | solution.py:435
  180.2 7.1 %collective-permute-start.2 = (bf16[64,2048]{1,0:T(8,128)(2,1)S(1)}, bf16[64,2048]{1,0:T(8,128)(2,1)S(1)}, u32[]{:S(2)}, u32[]{:S(2)}) collective-permute-start(bf16[64,2048]{1,0:T(8,128)(2,1)S(1)} %get-tuple-element.59), channel_id=1, source_target_pairs={{0,1},{1,2},{2,3},{3,4},{4,5},{5,6},{6,7},{8,9},{9,10},{10,11},{11... | collective-permute-start | bytes 786440 | tf_op jit(solution)/shard_map/ppermute | solution.py:433
  188.4 1.0 copy-start.20
  190.3 3.7 copy-start.25
  190.5 4.2 %copy-start.13 = (bf16[128,2688]{1,0:T(8,128)(2,1)S(1)}, bf16[128,2688]{1,0:T(8,128)(2,1)}, u32[]{:S(2)}) copy-start(bf16[128,2688]{1,0:T(8,128)(2,1)} %copy-done.12) | copy-start | bytes 2064388
  192.1 3.5 copy-start.22
  194.7 1.9 copy-start.37
  196.6 5.2 %copy-start.44 = (f32[128]{0:T(128)S(1)}, f32[128]{0:T(128)}, u32[]{:S(2)}) copy-start(f32[128]{0:T(128)} %copy-done.43) | copy-start | bytes 1540
  196.6 5.2 %copy-start.39 = (f32[128]{0:T(128)S(1)}, f32[128]{0:T(128)}, u32[]{:S(2)}) copy-start(f32[128]{0:T(128)} %copy-done.38) | copy-start | bytes 1540
  196.6 5.6 %copy-start.17 = (f32[128,1024]{1,0:T(8,128)S(1)}, f32[128,1024]{1,0:T(8,128)}, u32[]{:S(2)}) copy-start(f32[128,1024]{1,0:T(8,128)} %copy-done.16) | copy-start | bytes 1572868
  196.6 5.6 %copy-start.28 = (bf16[1,128,1024]{2,1,0:T(8,128)(2,1)S(1)}, bf16[1,128,1024]{2,1,0:T(8,128)(2,1)}, u32[]{:S(2)}) copy-start(bf16[1,128,1024]{2,1,0:T(8,128)(2,1)} %param.15) | copy-start | bytes 786436
  201.8 1.5 copy-start.31
  201.8 1.5 copy-start.32
  204.4 2.4 copy-start.8
  (6 other events, 4.5 us)

commit v3 on v2

--- a/solution.py
+++ b/solution.py
@@ -528,8 +528,8 @@
     row_max = jnp.max(scores, axis=-1, keepdims=True)
     exponent = jnp.exp(scores - row_max)
     row_sum = jnp.sum(exponent, axis=-1, keepdims=True)
-    log_total = row_max + jnp.log(row_sum)
-    attn_pb = (exponent / row_sum).astype(jnp.bfloat16)
+    attn_p = exponent / row_sum
+    attn_pb = attn_p.astype(jnp.bfloat16)
     attn_o = jnp.einsum("hts,shd->thd", attn_pb, value_wide, preferred_element_type=jnp.float32)
     attn_ob = attn_o.reshape(tok_rows, model_width).astype(jnp.bfloat16)
     residual = inputs + jnp.dot(attn_ob, full_out, preferred_element_type=jnp.float32)
@@ -559,17 +559,11 @@
         "te,de->td", grad_att_b, back_out, preferred_element_type=jnp.float32
     ).astype(jnp.bfloat16)
     grad_o_heads = grad_o_b.reshape(tok_rows, HEADS, HD)
-    scores_again = (
-        jnp.einsum("thd,shd->hts", q_heads, key_wide, preferred_element_type=jnp.float32)
-        * score_scale
-    )
-    scores_again = jnp.where(allowed[None], scores_again, masked_score)
-    prob_again = jnp.exp(scores_again - log_total)
     grad_prob = jnp.einsum(
         "thd,shd->hts", grad_o_heads, value_wide, preferred_element_type=jnp.float32
     )
-    delta_sum = jnp.sum(grad_prob * prob_again, axis=-1, keepdims=True)
-    grad_scores_b = (prob_again * (grad_prob - delta_sum)).astype(jnp.bfloat16)
+    delta_sum = jnp.sum(grad_prob * attn_p, axis=-1, keepdims=True)
+    grad_scores_b = (attn_p * (grad_prob - delta_sum)).astype(jnp.bfloat16)
     grad_query = (
         jnp.einsum("hts,shd->thd", grad_scores_b, key_wide, preferred_element_type=jnp.float32)
         * score_scale

time: 369 us -> 365 us (0.989)
  Pallas kernels: 245 us -> 240 us
    pallas_call x1, Pallas kernels: 143 us -> 138 us  [scatter_sums(): pl.pallas_call(functools.partial(scatter_kernel, n, edges), out_shape=jax...]
    unnamed x112 -> x120, local copies, waits for them, and re-layouts: 21.8 us -> 21.4 us
  transfers between devices with their start and end apart: 4 -> 4, of which waited for: 1 -> 2; matrix products, arithmetic and copies ran while one was open for 0% -> 1% of each run, Pallas kernels for 0% -> 0%
where the time goes in v3:
time: 365 us; the launch traced here: 364 us
  Pallas kernels  240 us (66%)
  local copies, waits for them, and re-layouts  47.3 us (13%)
  matrix products  45.5 us (12%)
  other arithmetic  15.2 us (4%)
  starting transfers between devices  12.8 us (4%)
    pallas_call x1, Pallas kernels, scatter_sums(): pl.pallas_call(functools.partial(scatter_kernel, n, edges), out_shape=jax...  138 us
    pallas_call x1, Pallas kernels, gather_weights(): pl.pallas_call(functools.partial(gather_kernel, n, count), out_shape=[jax...  102 us
    unnamed x120, local copies, waits for them, and re-layouts  21.4 us
    ppermute x2, starting transfers between devices, padded(): lax.ppermute(tail, axis, [(i, (i + 1) % count) for i in range(ends)])  9.79 us
  transfers between devices with their start and end apart: 4, of which 2 were waited for; matrix products, arithmetic and copies ran while one was open for 1% of the time, Pallas kernels for 0%

profile of v3, /device:TPU:0, one launch (start us, length us, event | category | flops | bytes accessed | tf_op | source)
XLA Modules:
  0.0 363.8 jit_solution(12016853840730125360)
XLA Ops:
  0.7 3.0 fusion.76
  3.7 1.8 copy.89
  5.5 1.7 copy.90
  7.3 1.2 copy-done.12
  8.5 1.2 pad.32.refs_3_
  9.7 1.8 copy.67
  11.8 1.2 copy-done.2
  13.2 1.4 copy-done.3
  14.6 101.5 %gather_weights.1 = (bf16[1024,3072]{1,0:T(8,128)(2,1)}, bf16[1024,1024]{1,0:T(8,128)(2,1)S(1)}, bf16[1024,2688]{1,0:T(8,128)(2,1)S(1)}, bf16[1024,2688]{1,0:T(8,128)(2,1)S(1)}, bf16[1024,2816]{1,0:T(8,128)(2,1)}) custom-call(bf16[256,3072]{1,0:T(8,128)(2,1)S(1)} %copy-done.3, bf16[256,1024]{1,0:T(8,128)(2,1)S(1)} %copy-done.4, ...), custom_call_target="tpu_custom_call" | custom-call | tf_op jit(solution)/shard_map/gather_weights/pallas_call | solution.py:228
  116.2 1.3 convert_bitcast_fusion.1
  118.3 5.5 %fusion.71 = f32[128,3072]{1,0:T(8,128)S(1)} fusion(bf16[1024,3072]{1,0:T(8,128)(2,1)} %get-tuple-element.13, bf16[1,128,1024]{2,1,0:T(8,128)(2,1)S(1)} %copy-done.7, f32[1024]{0:T(1024)S(1)} %get-tuple-element.43, f32[128]{0:T(128)S(1)} %fusion.61, f32[128]{0:T(128)S(1)} %broadcast_multiply_fusion.1), kind=kOutput, calls=%fused_computation.155 | convolution fusion | flops 805961728 | bytes 8131584 | tf_op jit(solution)/shard_map/dot_general | solution.py:505
  123.9 1.1 fusion.77
  125.0 1.2 copy.72
  126.2 2.0 copy.69
  129.0 1.8 subtract_convert_fusion.2
  131.1 3.0 collective-permute-start
  134.1 1.5 collective-permute-start.1
  136.4 1.3 collective-permute-done.1
  137.7 1.1 pad_maximum_fusion.1
  139.7 1.2 copy.73
  140.9 1.0 copy.71
  141.9 3.1 fusion.80
  145.1 2.3 convolution_convert_fusion.1
  148.4 1.0 fusion.82
  149.4 6.4 %multiply_convert_fusion.1 = (bf16[128,2688]{1,0:T(8,128)(2,1)S(1)}, f32[128,2688]{1,0:T(8,128)S(1)}, f32[128,2688]{1,0:T(8,128)S(1)}) fusion(f32[128,2688]{1,0:T(8,128)S(1)} %fusion.82, bf16[1024,2816]{1,0:T(8,128)(2,1)} %get-tuple-element.12, bf16[1,128,1024]{2,1,0:T(8,128)(2,1)S(1)} %copy-done.20), kind=kOutput, calls=%fused_computation.22 | convolution fusion | flops 727351296 | bytes 10584064 | tf_op jit(solution)/shard_map/dot_general | solution.py:550
  155.9 2.6 add_convert_fusion
  158.4 1.9 fusion.83
  160.3 2.5 multiply_reduce_fusion.1
  164.5 1.5 convolution_convert_fusion
  166.0 1.1 copy.75
  167.2 4.5 %multiply_reduce_fusion = (f32[16,128]{1,0:T(8,128)}, f32[16,128,256]{2,1,0:T(8,128)}) fusion(f32[16,128,256]{2,1,0:T(8,128)} %get-tuple-element.83, f32[16,128]{1,0:T(8,128)} %copy-done.37, bf16[128,16,64]{0,2,1:T(8,128)(2,1)S(1)} %bitcast.147, bf16[256,16,64]{0,2,1:T(8,128)(2,1)} %bitcast.144), kind=kOutput, calls=%fused_computation.15 | convolution fusion | flops 68679680 | bytes 4997120 | tf_op jit(solution)/shard_map/thd,shd->hts/dot_general | solution.py:562
  174.6 2.6 multiply_convert_fusion
  177.2 1.3 convolution_multiply_fusion
  178.5 1.6 copy.76
  180.3 6.8 %collective-permute-start.2 = (bf16[64,2048]{1,0:T(8,128)(2,1)S(1)}, bf16[64,2048]{1,0:T(8,128)(2,1)S(1)}, u32[]{:S(2)}, u32[]{:S(2)}) collective-permute-start(bf16[64,2048]{1,0:T(8,128)(2,1)S(1)} %get-tuple-element.59), channel_id=1, source_target_pairs={{0,1},{1,2},{2,3},{3,4},{4,5},{5,6},{6,7},{8,9},{9,10},{10,11},{11... | collective-permute-start | bytes 786440 | tf_op jit(solution)/shard_map/ppermute | solution.py:433
  187.1 1.5 collective-permute-start.3
  188.6 1.3 fusion.19
  195.5 1.9 constant_dynamic-update-slice_fusion.5
  197.3 5.1 %fusion.51 = (f32[128]{0:T(128)S(1)}, f32[128,1024]{1,0:T(8,128)S(1)}) fusion(bf16[1,128,1024]{2,1,0:T(8,128)(2,1)S(1)} %copy-done.7, f32[1024]{0:T(1024)S(1)} %get-tuple-element.43, f32[128]{0:T(128)S(1)} %copy-done.36, bf16[1024,3072]{1,0:T(8,128)(2,1)} %get-tuple-element.13, bf16[128,1024]{1,0:T(8,128)(2,1)S(1)} %get-tuple-element.47, ...), kind=kOutput, calls=%fused_computation.81 | convolution fusion | flops 808320896 | bytes 7869440 | tf_op jit(solution)/shard_map/te,de->td/dot_general | solution.py:598
  203.8 1.1 fusion.70
  205.1 1.3 copy.85.at_ref
  209.4 2.5 constant_dynamic-update-slice_fusion.1
  212.5 138.1 %scatter_sums.1 = f32[32,12288]{1,0:T(8,128)} custom-call(bf16[4,1024,128]{2,1,0:T(8,128)(2,1)} %copy.85.at_ref, bf16[128,12288]{1,0:T(8,128)(2,1)} %constant_dynamic-update-slice_fusion.b_ref, bf16[1024,128]{1,0:T(8,128)(2,1)} %pad.38.gcol_ref), custom_call_target="tpu_custom_call" | custom-call | tf_op jit(solution)/shard_map/scatter_sums/pallas_call | solution.py:398
  350.6 2.0 slice_bitcast_fusion
  352.6 1.8 slice.137
  354.3 1.6 slice.138
  356.7 1.4 copy.86
  358.7 5.2 %fusion.26 = bf16[1,128,1024]{2,1,0:T(8,128)(2,1)} fusion(f32[128,1024]{1,0:T(8,128)S(1)} %get-tuple-element.85, bf16[128,2688]{1,0:T(8,128)(2,1)S(1)} %get-tuple-element.45, bf16[1024,2816]{1,0:T(8,128)(2,1)} %get-tuple-element.12), kind=kOutput, calls=%fused_computation.48 | convolution fusion | flops 704905216 | bytes 6979584 | tf_op jit(solution)/shard_map/tf,df->td/dot_general | solution.py:543
  (170 shorter events, 21.5 us)
Async XLA Ops:
  7.2 1.3 copy-start.12
  9.7 1.8 copy-start.46
  11.7 1.3 copy-start.2
  11.7 1.5 copy-start.4
  13.2 1.4 copy-start.3
  116.1 7.7 %copy-start = (bf16[1024,2688]{1,0:T(8,128)(2,1)}, bf16[1024,2688]{1,0:T(8,128)(2,1)S(1)}, u32[]{:S(2)}) copy-start(bf16[1024,2688]{1,0:T(8,128)(2,1)S(1)} %get-tuple-element.16) | copy-start | bytes 16515076
  116.1 7.7 %copy-start.1 = (bf16[1024,2688]{1,0:T(8,128)(2,1)}, bf16[1024,2688]{1,0:T(8,128)(2,1)S(1)}, u32[]{:S(2)}) copy-start(bf16[1024,2688]{1,0:T(8,128)(2,1)S(1)} %get-tuple-element.15) | copy-start | bytes 16515076
  116.1 1.8 copy-start.7
  118.1 5.8 %copy-start.35 = (f32[128]{0:T(128)}, f32[128]{0:T(128)S(1)}, u32[]{:S(2)}) copy-start(f32[128]{0:T(128)S(1)} %broadcast_multiply_fusion.1) | copy-start | bytes 1540
  118.3 5.6 %copy-start.47 = (f32[128]{0:T(128)}, f32[128]{0:T(128)S(1)}, u32[]{:S(2)}) copy-start(f32[128]{0:T(128)S(1)} %fusion.50) | copy-start | bytes 1540
  118.3 5.6 %copy-start.40 = (f32[128]{0:T(128)}, f32[128]{0:T(128)S(1)}, u32[]{:S(2)}) copy-start(f32[128]{0:T(128)S(1)} %fusion.61) | copy-start | bytes 1540
  129.0 1.9 copy-start.32
  130.9 4.7 %copy-start.43 = (s32[1,1024]{1,0:T(1,128)S(1)}, s32[1,1024]{1,0:T(1,128)}, u32[]{:S(2)}) copy-start(s32[1,1024]{1,0:T(1,128)} %param.9) | copy-start | bytes 12292
  131.1 5.3 %collective-permute-start = (bf16[64,2048]{1,0:T(8,128)(2,1)S(1)}, bf16[64,2048]{1,0:T(8,128)(2,1)}, u32[]{:S(2)}, u32[]{:S(2)}) collective-permute-start(bf16[64,2048]{1,0:T(8,128)(2,1)S(1)} %get-tuple-element.71), channel_id=1, source_target_pairs={{0,1},{1,2},{2,3},{3,4},{4,5},{5,6},{6,7},{8,9},{9,10},{10,11},{11... | collective-permute-start | bytes 786440 | tf_op jit(solution)/shard_map/ppermute | solution.py:433
  134.1 3.6 collective-permute-start.1
  140.9 4.1 %copy-start.24 = (bf16[256,1024]{0,1:T(8,128)(2,1)}, bf16[256,1024]{0,1:T(8,128)(2,1)S(1)}, u32[]{:S(2)}) copy-start(bf16[256,1024]{0,1:T(8,128)(2,1)S(1)} %copy.73) | copy-start | bytes 1572868
  141.9 3.1 copy-start.31
  145.0 2.3 copy-start.37
  145.0 3.3 slice-start.2
  145.1 3.3 slice-start.3
  148.3 7.5 %slice-start = ((s8[5505024]{0:T(1024)(128)(4,1)}), s8[4194304]{0:T(1024)(128)(4,1)S(1)}, s32[]{:S(2)}) async-start(s8[5505024]{0:T(1024)(128)(4,1)} %bitcast.123), calls=%async_computation | async-start | bytes 8388608
  149.3 6.5 %copy-start.5 = (f32[128,2688]{1,0:T(8,128)}, f32[128,2688]{1,0:T(8,128)S(1)}, u32[]{:S(2)}) copy-start(f32[128,2688]{1,0:T(8,128)S(1)} %fusion.82) | copy-start | bytes 4128772
  149.4 6.5 %slice-start.1 = ((s8[5505024]{0:T(1024)(128)(4,1)}), s8[1310720]{0:T(1024)(128)(4,1)S(1)}, s32[]{:S(2)}) async-start(s8[5505024]{0:T(1024)(128)(4,1)} %bitcast.123), calls=%async_computation.1 | async-start | bytes 2621440
  155.8 2.6 copy-start.13
  155.8 4.5 %copy-start.16 = (bf16[128,2688]{1,0:T(8,128)(2,1)}, bf16[128,2688]{1,0:T(8,128)(2,1)S(1)}, u32[]{:S(2)}) copy-start(bf16[128,2688]{1,0:T(8,128)(2,1)S(1)} %get-tuple-element.50) | copy-start | bytes 2064388
  158.4 1.9 copy-start.10
  167.1 4.6 %copy-start.22 = (f32[16,128,256]{2,1,0:T(8,128)S(1)}, f32[16,128,256]{2,1,0:T(8,128)}, u32[]{:S(2)}) copy-start(f32[16,128,256]{2,1,0:T(8,128)} %get-tuple-element.83) | copy-start | bytes 6291460
  167.2 4.6 %copy-start.38 = (f32[16,128]{1,0:T(8,128)S(1)}, f32[16,128]{1,0:T(8,128)}, u32[]{:S(2)}) copy-start(f32[16,128]{1,0:T(8,128)} %copy-done.37) | copy-start | bytes 24580
  171.7 1.6 copy-start.29
  174.5 2.6 copy-start.30
  177.2 1.3 copy-start.8
  180.1 8.5 %copy-start.42 = (bf16[1024]{0:T(1024)(128)(2,1)S(1)}, bf16[1024]{0:T(1024)(128)(2,1)}, u32[]{:S(2)}) copy-start(bf16[1024]{0:T(1024)(128)(2,1)} %get-tuple-element.38) | copy-start | bytes 6148
  180.1 8.6 %copy-start.9 = (bf16[16,128,256]{2,1,0:T(8,128)(2,1)S(1)}, bf16[16,128,256]{2,1,0:T(8,128)(2,1)}, u32[]{:S(2)}) copy-start(bf16[16,128,256]{2,1,0:T(8,128)(2,1)} %copy-done.8) | copy-start | bytes 3145732
  180.1 8.6 %copy-start.25 = (bf16[256,1024]{0,1:T(8,128)(2,1)S(1)}, bf16[256,1024]{0,1:T(8,128)(2,1)}, u32[]{:S(2)}) copy-start(bf16[256,1024]{0,1:T(8,128)(2,1)} %copy-done.24) | copy-start | bytes 1572868
  180.3 9.6 %collective-permute-start.2 = (bf16[64,2048]{1,0:T(8,128)(2,1)S(1)}, bf16[64,2048]{1,0:T(8,128)(2,1)S(1)}, u32[]{:S(2)}, u32[]{:S(2)}) collective-permute-start(bf16[64,2048]{1,0:T(8,128)(2,1)S(1)} %get-tuple-element.59), channel_id=1, source_target_pairs={{0,1},{1,2},{2,3},{3,4},{4,5},{5,6},{6,7},{8,9},{9,10},{10,11},{11... | collective-permute-start | bytes 786440 | tf_op jit(solution)/shard_map/ppermute | solution.py:433
  187.1 3.4 collective-permute-start.3
  193.7 3.7 %copy-start.36 = (f32[128]{0:T(128)S(1)}, f32[128]{0:T(128)}, u32[]{:S(2)}) copy-start(f32[128]{0:T(128)} %copy-done.35) | copy-start | bytes 1540
  197.3 5.1 %copy-start.48 = (f32[128]{0:T(128)S(1)}, f32[128]{0:T(128)}, u32[]{:S(2)}) copy-start(f32[128]{0:T(128)} %copy-done.47) | copy-start | bytes 1540
  197.3 5.1 %copy-start.41 = (f32[128]{0:T(128)S(1)}, f32[128]{0:T(128)}, u32[]{:S(2)}) copy-start(f32[128]{0:T(128)} %copy-done.40) | copy-start | bytes 1540
  202.4 1.4 copy-start.21
  202.4 1.4 copy-start.45
  203.0 1.9 copy-start.26
  203.1 1.9 copy-start.27
  205.1 1.4 copy-start.19
  205.1 2.1 copy-start.11
  205.1 3.0 copy-start.17
  207.2 1.9 copy-start.6
  207.2 2.2 copy-start.14
  (10 other events, 8.9 us)
